TPU v7x, 256 devices: a whole 4x4x8 slice. The times are simulated.
256 devices in a mesh: gx: 4 (over x), gy: 4 (over y), gz: 16 (over z, core).
Axes of the slice: x: 4, y: 4, z: 8, core: 2. Of those that a mesh axis runs over, the one named last changes fastest.
Arguments:
- leaf_offsets: float32 [3, 524288], P(None, ('gx', 'gy', 'gz')), may hold values from -0.5 to 0.5
- latent_charges: float32 [524288], P(('gx', 'gy', 'gz')), may hold values from -0.2 to 0.2
- atom_counts: int32 [8192], P(('gx', 'gy', 'gz')), may hold values from 1 to 64
- near_boxes: int32 [26, 8192], P(None, ('gx', 'gy', 'gz')), may hold values from -1 to 8191, as said below
- far_slots: int32 [189, 8192], P(None, ('gx', 'gy', 'gz')), may hold values from -1 to 95, as said below
- branch_slots: int32 [256, 8, 8], P(('gx', 'gy', 'gz')), may hold values from 0 to 87, as said below
- far_operators: bfloat16 [165, 31185], replicated, may hold values from -0.5 to 0.5
Outputs:
- potential: float32 [524288], P(('gx', 'gy', 'gz'))
Inputs may be any that keep to these rules, and one draw needn't show every extreme that they name: `near_boxes`: an entry names a box owned by the same device as box g or by its neighbour one step along gz (never past the ends of gz), lying within 8 boxes of the device's own range; or it is -1. `far_slots`: an entry is -1 or a slot of the held set of the device that owns box g. branch_slots[d, k, j] is below 32 + k * 8: a slot that device d holds before section k.
All inputs are finite; a program needn't handle non-finite values.
Results may differ from a plain program's by a relative error of at most 0.0017.
Values may be sent and summed in bfloat16 or wider, within the bound.
A program may use at most 128 MiB of HBM per device.

v0:
```python
import math

import jax
import jax.numpy as jnp
import numpy as np
from jax import lax
from jax.sharding import PartitionSpec as P

ORDER = 8
HALO = 8


soften = 0.25


def swapped(shard, axis, apart):
    return lax.ppermute(shard, axis, [(i, i ^ 1 << apart) for i in range(lax.axis_size(axis))])


def extended_2(shard, sides, width):
    for axis, dim in sides:
        size, length = (lax.axis_size(axis), shard.shape[dim])
        up = [(i, (i + 1) % size) for i in range(size - 1)]
        down = [(j, i) for i, j in up]
        last = lax.slice_in_dim(shard, length - width, length, axis=dim)
        leading = lax.slice_in_dim(shard, 0, width, axis=dim)
        before = lax.ppermute(last, axis, up)
        after = lax.ppermute(leading, axis, down)
        shard = jnp.concatenate([before, shard, after], axis=dim)
    return shard


def term_table():
    listed = [
        (first_exp, second_exp, degree - first_exp - second_exp)
        for degree in range(ORDER + 1)
        for first_exp in range(degree, -1, -1)
        for second_exp in range(degree - first_exp, -1, -1)
    ]
    return np.array(listed, dtype=np.int32)


def monomials(scaled):
    table_np = term_table()
    stacked = [jnp.ones_like(scaled)]
    for degree in range(ORDER):
        stacked.append(stacked[-1] * scaled)
    powers = jnp.stack(stacked, 0)
    return powers[table_np[:, 0], 0] * powers[table_np[:, 1], 1] * powers[table_np[:, 2], 2]


def shift_table():
    listed = [
        (first_step, second_step, third_step)
        for first_step in (-1, 0, 1)
        for second_step in (-1, 0, 1)
        for third_step in (-1, 0, 1)
        if first_step != 0 or second_step != 0 or third_step != 0
    ]
    return np.array(listed, dtype=np.float32).T


def near_block(target, source_pos, source_q, shifts):
    dist_sq = soften * soften
    for axis_num in range(3):
        spacing = (
            shifts[axis_num][:, None, None, None]
            + source_pos[axis_num][:, :, None, :]
            - target[axis_num][None, :, :, None]
        )
        dist_sq = dist_sq + spacing * spacing
    return jnp.sum(source_q[:, :, None, :] * lax.rsqrt(dist_sq), axis=(0, 3))


def self_block(target, target_q):
    dist_sq = soften * soften
    for axis_num in range(3):
        spacing = target[axis_num][:, None, :] - target[axis_num][:, :, None]
        dist_sq = dist_sq + spacing * spacing
    slot_count = target.shape[-1]
    distinct = jnp.arange(slot_count)[:, None] != jnp.arange(slot_count)[None, :]
    return jnp.sum(
        jnp.where(distinct[None], target_q[:, None, :] * lax.rsqrt(dist_sq), 0.0), axis=2
    )


def local(
    leaf_offsets, latent_charges, atom_counts, near_boxes, far_slots, branch_slots, far_operators
):
    box_count = atom_counts.shape[0]
    slot_count = latent_charges.shape[0] // box_count
    filled = jnp.arange(slot_count, dtype=jnp.int32)[None, :] < atom_counts[:, None]
    masked = jnp.where(filled, latent_charges.reshape(box_count, slot_count), 0.0)
    term_values = monomials(2.0 * leaf_offsets)
    term_count = term_values.shape[0]
    term_values = term_values.reshape(term_count, box_count, slot_count)
    multipoles = jnp.einsum(
        "kbs,bs->kb", term_values, masked, precision=lax.Precision.HIGHEST
    ).astype(jnp.bfloat16)
    device = lax.axis_index(("gx", "gy", "gz"))
    held_terms = multipoles
    section_idx = 0
    for bit_num in range(lax.axis_size("gz").bit_length() - 1):
        payload = jnp.take(held_terms, branch_slots[0, section_idx], axis=1)
        held_terms = jnp.concatenate([held_terms, swapped(payload, "gz", bit_num)], axis=1)
        section_idx += 1
    for bit_num in range(lax.axis_size("gy").bit_length() - 1):
        payload = jnp.take(held_terms, branch_slots[0, section_idx], axis=1)
        held_terms = jnp.concatenate([held_terms, swapped(payload, "gy", bit_num)], axis=1)
        section_idx += 1
    for bit_num in range(lax.axis_size("gx").bit_length() - 1):
        payload = jnp.take(held_terms, branch_slots[0, section_idx], axis=1)
        held_terms = jnp.concatenate([held_terms, swapped(payload, "gx", bit_num)], axis=1)
        section_idx += 1
    list_count = far_slots.shape[0]
    far_present = far_slots >= 0
    columns = jnp.take(held_terms, jnp.clip(far_slots, 0, held_terms.shape[1] - 1), axis=1)
    columns = jnp.where(far_present[None], columns, jnp.zeros((), jnp.bfloat16))
    operators = far_operators.reshape(term_count, list_count, term_count)
    local_terms = jnp.einsum("klt,tlb->kb", operators, columns, preferred_element_type=jnp.float32)
    far_field_sum = jnp.einsum(
        "kb,kbs->bs", local_terms, term_values, precision=lax.Precision.HIGHEST
    )
    halo_boxes = HALO
    packed = jnp.concatenate([leaf_offsets, masked.reshape(1, -1)], axis=0)
    extended = extended_2(packed, (("gz", 1),), halo_boxes * slot_count)
    ext_boxes = extended.reshape(4, box_count + 2 * halo_boxes, slot_count)
    base_box = device * box_count - halo_boxes
    local_ids = jnp.clip(near_boxes - base_box, 0, box_count + 2 * halo_boxes - 1)
    near_present = near_boxes >= 0
    positions = leaf_offsets.reshape(3, box_count, slot_count)
    shifts = shift_table()
    block_len = math.gcd(box_count, 16)

    def one_block(block_id):
        first_box = block_id * block_len
        target = lax.dynamic_slice_in_dim(positions, first_box, block_len, 1)
        target_q = lax.dynamic_slice_in_dim(masked, first_box, block_len, 0)
        block_ids = lax.dynamic_slice_in_dim(local_ids, first_box, block_len, 1)
        block_present = lax.dynamic_slice_in_dim(near_present, first_box, block_len, 1)
        source_pos = ext_boxes[:3][:, block_ids]
        source_q = jnp.where(block_present[:, :, None], ext_boxes[3][block_ids], 0.0)
        return self_block(target, target_q) + near_block(target, source_pos, source_q, shifts)

    near_field_sum = lax.map(
        one_block, jnp.arange(box_count // block_len, dtype=jnp.int32)
    ).reshape(box_count, slot_count)
    potential = jnp.where(filled, near_field_sum + far_field_sum, 0.0)
    return potential.reshape(-1)


def solution(mesh):
    in_specs = (
        P(None, ("gx", "gy", "gz")),
        P(("gx", "gy", "gz")),
        P(("gx", "gy", "gz")),
        P(None, ("gx", "gy", "gz")),
        P(None, ("gx", "gy", "gz")),
        P(("gx", "gy", "gz"), None, None),
        P(),
    )
    out_specs = P(("gx", "gy", "gz"))
    return jax.shard_map(local, mesh=mesh, in_specs=in_specs, out_specs=out_specs, check_vma=False)
```

profile of v0, /device:TPU:32, one launch (start us, length us, event | category | flops | bytes accessed | tf_op | source)
XLA Modules:
  0.0 207.2 jit_solution(6535297377824247839)
XLA Ops:
  2.1 1.3 pad_maximum_fusion.5
  3.4 1.9 collective-permute-start
  5.4 3.6 %collective-permute-start.1 = (f32[4,512]{1,0:T(4,128)}, f32[4,512]{1,0:T(4,128)}, u32[]{:S(2)}, u32[]{:S(2)}) collective-permute-start(f32[4,512]{1,0:T(4,128)} %get-tuple-element.123), channel_id=1, source_target_pairs={{1,0},{2,1},{3,2},{4,3},{5,4},{6,5},{7,6},{8,7},{9,8},{10,9},{11,1... | collective-permute-start | bytes 24584 | tf_op jit(solution)/shard_map/ppermute | solution.py:28
  9.0 1.6 compare_and_fusion.1
  10.6 1.6 fusion.33
  20.5 4.5 %gather_fusion.4 = f32[165,2048]{1,0:T(8,128)S(1)} fusion(f32[9,3,2048]{2,1,0:T(4,128)S(1)} %constant_dynamic-update-slice_fusion, s32[165]{0:T(256)} %constant.292), kind=kCustom, calls=%fused_computation.4 | custom fusion | bytes 2704680 | tf_op jit(solution)/shard_map/gather | solution.py:49
  25.1 5.7 %gather_fusion.3 = f32[165,2048]{1,0:T(8,128)} fusion(f32[9,3,2048]{2,1,0:T(4,128)S(1)} %constant_dynamic-update-slice_fusion, s32[165]{0:T(256)S(1)} %copy-done.3), kind=kCustom, calls=%fused_computation.3 | custom fusion | bytes 2704680 | tf_op jit(solution)/shard_map/gather | solution.py:49
  30.8 6.0 %gather_fusion.2 = f32[165,2048]{1,0:T(8,128)} fusion(f32[9,3,2048]{2,1,0:T(4,128)S(1)} %constant_dynamic-update-slice_fusion, s32[165]{0:T(256)S(1)} %copy-done.2), kind=kCustom, calls=%fused_computation.2 | custom fusion | bytes 2704680 | tf_op jit(solution)/shard_map/gather | solution.py:49
  36.8 2.0 multiply_multiply_fusion
  39.8 1.1 fusion.38
  47.4 3.3 %collective-permute-done.3 = bf16[165,8]{0,1:T(8,128)(2,1)S(1)} collective-permute-done((bf16[165,8]{0,1:T(8,128)(2,1)S(1)}, bf16[165,8]{0,1:T(8,128)(2,1)S(1)}, u32[]{:S(2)}, u32[]{:S(2)}) %collective-permute-start.3) | collective-permute-done | bytes 2672 | tf_op jit(solution)/shard_map/ppermute | solution.py:17
  51.4 4.5 %collective-permute-start.4 = (bf16[165,8]{0,1:T(8,128)(2,1)S(1)}, bf16[165,8]{0,1:T(8,128)(2,1)S(1)}, u32[]{:S(2)}, u32[]{:S(2)}) collective-permute-start(bf16[165,8]{0,1:T(8,128)(2,1)S(1)} %select_bitcast_fusion.5), channel_id=1, source_target_pairs={{0,4},{1,5},{2,6},{3,7},{4,0},{5,1},{6,2},{7,3},{8,12},{9,13},{10,... | collective-permute-start | bytes 7928 | tf_op jit(solution)/shard_map/ppermute | solution.py:17
  55.9 1.6 collective-permute-done.4
  58.2 4.7 %collective-permute-start.5 = (bf16[165,8]{0,1:T(8,128)(2,1)S(1)}, bf16[165,8]{0,1:T(8,128)(2,1)S(1)}, u32[]{:S(2)}, u32[]{:S(2)}) collective-permute-start(bf16[165,8]{0,1:T(8,128)(2,1)S(1)} %select_bitcast_fusion.4), channel_id=1, source_target_pairs={{0,8},{1,9},{2,10},{3,11},{4,12},{5,13},{6,14},{7,15},{8,0},{9,1},... | collective-permute-start | bytes 7928 | tf_op jit(solution)/shard_map/ppermute | solution.py:17
  62.8 2.9 %collective-permute-done.5 = bf16[165,8]{0,1:T(8,128)(2,1)S(1)} collective-permute-done((bf16[165,8]{0,1:T(8,128)(2,1)S(1)}, bf16[165,8]{0,1:T(8,128)(2,1)S(1)}, u32[]{:S(2)}, u32[]{:S(2)}) %collective-permute-start.5) | collective-permute-done | bytes 2672 | tf_op jit(solution)/shard_map/ppermute | solution.py:17
  66.4 1.6 collective-permute-start.6
  68.0 2.0 collective-permute-done.6
  70.7 3.2 %collective-permute-start.7 = (bf16[165,8]{0,1:T(8,128)(2,1)S(1)}, bf16[165,8]{0,1:T(8,128)(2,1)S(1)}, u32[]{:S(2)}, u32[]{:S(2)}) collective-permute-start(bf16[165,8]{0,1:T(8,128)(2,1)S(1)} %select_bitcast_fusion.2), channel_id=1, source_target_pairs={{0,32},{16,48},{32,0},{48,16},{1,33},{17,49},{33,1},{49,17},{2,34}... | collective-permute-start | bytes 7928 | tf_op jit(solution)/shard_map/ppermute | solution.py:17
  74.3 44.8 %reshape.387 = bf16[165,189,165]{2,1,0:T(8,128)(2,1)} reshape(bf16[165,31185]{1,0:T(8,128)(2,1)} %param.24) | data formatting | bytes 20582100 | tf_op jit(solution)/shard_map/reshape | solution.py:119
  119.8 1.5 collective-permute-start.8
  122.2 1.3 collective-permute-done.8
  124.1 3.3 %collective-permute-start.9 = (bf16[165,8]{0,1:T(8,128)(2,1)S(1)}, bf16[165,8]{0,1:T(8,128)(2,1)S(1)}, u32[]{:S(2)}, u32[]{:S(2)}) collective-permute-start(bf16[165,8]{0,1:T(8,128)(2,1)S(1)} %select_bitcast_fusion), channel_id=1, source_target_pairs={{0,128},{64,192},{128,0},{192,64},{1,129},{65,193},{129,1},{193,65... | collective-permute-start | bytes 7928 | tf_op jit(solution)/shard_map/ppermute | solution.py:17
  127.4 25.9 %while.11 = (s32[]{:T(128)}, f32[2,16,64]{2,1,0:T(8,128)S(1)}, s32[2]{0:T(128)S(1)}, f32[32,64]{1,0:T(8,128)S(1)}, f32[3,32,64]{2,1,0:T(8,128)S(1)}, /*index=5*/...) while((s32[]{:T(128)}, f32[2,16,64]{2,1,0:T(8,128)S(1)}, ...), condition=%wide.region_3.4_spmd.clone, body=%wide.region_0.0_spmd.sunk.clone.sunk | while | flops 19641576 | bytes 3011755 | solution.py:145
  129.7 1.1 gather_fusion.1
  130.8 2.2 %gather_fusion = f32[416,3,64]{2,1,0:T(4,128)S(1)} fusion(f32[3,48,64]{2,0,1:T(4,128)S(1)} %bitcast.161, s32[1024]{0:T(1024)S(1)} %pad_clamp_fusion.11), kind=kCustom, calls=%fused_computation.1.clone.1 | custom fusion | bytes 640640 | tf_op jit(solution)/shard_map/while/body/eval_jaxpr/gather | solution.py:141
  133.8 6.6 %multiply_reduce_fusion.2 = f32[16,64]{1,0:T(8,128)S(1)} fusion(f32[16,64]{1,0:T(8,128)S(1)} %get-tuple-element.234, f32[26,16,64]{2,1,0:T(8,128)S(1)} %get-tuple-element.239, f32[16,64]{1,0:T(8,128)S(1)} %get-tuple-element.235, f32[26,16,64]{2,1,0:T(8,128)S(1)} %get-tuple-element.240, f32[16,64]{1,0:T(8,128)S(1)} %get-tuple-element.236, ...), kind=kLoop, calls=%fused_computation.14.clone.1 | loop fusion | flops 18742272 | bytes 442368 | tf_op jit(solution)/shard_map/while/body/eval_jaxpr/reduce_sum | solution.py:72
  142.6 1.1 gather_fusion.1
  143.8 2.2 %gather_fusion = f32[416,3,64]{2,1,0:T(4,128)S(1)} fusion(f32[3,48,64]{2,0,1:T(4,128)S(1)} %bitcast.161, s32[1024]{0:T(1024)S(1)} %pad_clamp_fusion.11), kind=kCustom, calls=%fused_computation.1.clone.1 | custom fusion | bytes 640640 | tf_op jit(solution)/shard_map/while/body/eval_jaxpr/gather | solution.py:141
  146.7 6.6 %multiply_reduce_fusion.2 = f32[16,64]{1,0:T(8,128)S(1)} fusion(f32[16,64]{1,0:T(8,128)S(1)} %get-tuple-element.234, f32[26,16,64]{2,1,0:T(8,128)S(1)} %get-tuple-element.239, f32[16,64]{1,0:T(8,128)S(1)} %get-tuple-element.235, f32[26,16,64]{2,1,0:T(8,128)S(1)} %get-tuple-element.240, f32[16,64]{1,0:T(8,128)S(1)} %get-tuple-element.236, ...), kind=kLoop, calls=%fused_computation.14.clone.1 | loop fusion | flops 18742272 | bytes 442368 | tf_op jit(solution)/shard_map/while/body/eval_jaxpr/reduce_sum | solution.py:72
  153.3 22.1 %gather_fusion.13 = bf16[6048,165]{1,0:T(8,128)(2,1)S(1)} fusion(bf16[165,96]{0,1:T(8,128)(2,1)S(1)} %constant_dynamic-update-slice_fusion.35, s32[6144]{0:T(1024)S(1)} %pad_clamp_fusion.1), kind=kCustom, calls=%fused_computation.13 | custom fusion | bytes 4015872 | tf_op jit(solution)/shard_map/jit(_take)/gather | solution.py:117
  175.4 29.2 %fusion.9 = f32[165,32,1]{0,1,2:T(8,128)S(1)} fusion(bf16[165,189,165]{2,1,0:T(8,128)(2,1)} %reshape.387, bf16[189,32,165]{2,1,0:T(8,128)(2,1)S(1)} %bitcast.167, pred[189,32]{1,0:T(8,128)(4,1)S(1)} %copy.25, pred[189,32]{1,0:T(8,128)(4,1)S(1)} %copy.26), kind=kOutput, calls=%fused_computation.40 | convolution fusion | flops 331309440 | bytes 12320106 | tf_op jit(solution)/shard_map/klt,tlb->kb/dot_general | solution.py:120
  204.6 1.8 fusion.20
  (151 shorter events, 28.2 us)
Async XLA Ops:
  3.4 117.9 %collective-permute-start = (f32[4,512]{1,0:T(4,128)}, f32[4,512]{1,0:T(4,128)}, u32[]{:S(2)}, u32[]{:S(2)}) collective-permute-start(f32[4,512]{1,0:T(4,128)} %get-tuple-element.122), channel_id=1, source_target_pairs={{0,1},{1,2},{2,3},{3,4},{4,5},{5,6},{6,7},{7,8},{8,9},{9,10},{10,1... | collective-permute-start | bytes 24584 | tf_op jit(solution)/shard_map/ppermute | solution.py:27
  5.4 116.0 %collective-permute-start.1 = (f32[4,512]{1,0:T(4,128)}, f32[4,512]{1,0:T(4,128)}, u32[]{:S(2)}, u32[]{:S(2)}) collective-permute-start(f32[4,512]{1,0:T(4,128)} %get-tuple-element.123), channel_id=1, source_target_pairs={{1,0},{2,1},{3,2},{4,3},{5,4},{6,5},{7,6},{8,7},{9,8},{10,9},{11,1... | collective-permute-start | bytes 24584 | tf_op jit(solution)/shard_map/ppermute | solution.py:28
  20.5 4.6 %copy-start.3 = (s32[165]{0:T(256)S(1)}, s32[165]{0:T(256)}, u32[]{:S(2)}) copy-start(s32[165]{0:T(256)} %constant.284) | copy-start | bytes 1984
  25.1 5.8 %copy-start.2 = (s32[165]{0:T(256)S(1)}, s32[165]{0:T(256)}, u32[]{:S(2)}) copy-start(s32[165]{0:T(256)} %constant.276) | copy-start | bytes 1984
  38.8 2.8 %copy-start.22 = (pred[8]{0:T(512)(128)(4,1)S(1)}, pred[8]{0:T(512)(128)(4,1)}, u32[]{:S(2)}) copy-start(pred[8]{0:T(512)(128)(4,1)} %get-tuple-element.136) | copy-start | bytes 28
  38.8 3.2 %copy-start.5 = (s32[189,32]{0,1:T(8,128)S(1)}, s32[189,32]{0,1:T(8,128)}, u32[]{:S(2)}) copy-start(s32[189,32]{0,1:T(8,128)} %param.22) | copy-start | bytes 72580
  39.7 2.4 %copy-start = (f32[165,2048]{0,1:T(8,128)}, f32[165,2048]{0,1:T(8,128)S(1)}, u32[]{:S(2)}) copy-start(f32[165,2048]{0,1:T(8,128)S(1)} %copy.27) | copy-start | bytes 4055044
  39.7 6.7 %copy-start.21 = (s32[8]{0:T(128)S(1)}, s32[8]{0:T(128)}, u32[]{:S(2)}) copy-start(s32[8]{0:T(128)} %get-tuple-element.143) | copy-start | bytes 100
  39.7 7.3 %copy-start.20 = (pred[8]{0:T(512)(128)(4,1)S(1)}, pred[8]{0:T(512)(128)(4,1)}, u32[]{:S(2)}) copy-start(pred[8]{0:T(512)(128)(4,1)} %get-tuple-element.135) | copy-start | bytes 28
  39.7 11.6 %copy-start.19 = (pred[8]{0:T(512)(128)(4,1)S(1)}, pred[8]{0:T(512)(128)(4,1)}, u32[]{:S(2)}) copy-start(pred[8]{0:T(512)(128)(4,1)} %get-tuple-element.134) | copy-start | bytes 28
  39.7 18.4 %copy-start.18 = (pred[8]{0:T(512)(128)(4,1)S(1)}, pred[8]{0:T(512)(128)(4,1)}, u32[]{:S(2)}) copy-start(pred[8]{0:T(512)(128)(4,1)} %get-tuple-element.133) | copy-start | bytes 28
  39.7 26.6 %copy-start.16 = (pred[8]{0:T(512)(128)(4,1)S(1)}, pred[8]{0:T(512)(128)(4,1)}, u32[]{:S(2)}) copy-start(pred[8]{0:T(512)(128)(4,1)} %get-tuple-element.132) | copy-start | bytes 28
  39.7 28.3 %copy-start.17 = (s32[8]{0:T(128)S(1)}, s32[8]{0:T(128)}, u32[]{:S(2)}) copy-start(s32[8]{0:T(128)} %get-tuple-element.144) | copy-start | bytes 100
  39.7 30.9 %copy-start.14 = (pred[8]{0:T(512)(128)(4,1)S(1)}, pred[8]{0:T(512)(128)(4,1)}, u32[]{:S(2)}) copy-start(pred[8]{0:T(512)(128)(4,1)} %get-tuple-element.131) | copy-start | bytes 28
  39.7 34.2 %copy-start.15 = (s32[8]{0:T(128)S(1)}, s32[8]{0:T(128)}, u32[]{:S(2)}) copy-start(s32[8]{0:T(128)} %get-tuple-element.145) | copy-start | bytes 100
  39.7 34.2 %copy-start.4 = (f32[3,2048]{1,0:T(4,128)S(1)}, f32[3,2048]{1,0:T(4,128)}, u32[]{:S(2)}) copy-start(f32[3,2048]{1,0:T(4,128)} %param.18) | copy-start | bytes 73732
  41.7 4.7 %collective-permute-start.2 = (bf16[165,8]{0,1:T(8,128)(2,1)S(1)}, bf16[165,8]{0,1:T(8,128)(2,1)S(1)}, u32[]{:S(2)}, u32[]{:S(2)}) collective-permute-start(bf16[165,8]{0,1:T(8,128)(2,1)S(1)} %select_bitcast_fusion.7), channel_id=1, source_target_pairs={{0,1},{1,0},{2,3},{3,2},{4,5},{5,4},{6,7},{7,6},{8,9},{9,8},{10,11... | collective-permute-start | bytes 7928 | tf_op jit(solution)/shard_map/ppermute | solution.py:17
  47.1 3.6 %collective-permute-start.3 = (bf16[165,8]{0,1:T(8,128)(2,1)S(1)}, bf16[165,8]{0,1:T(8,128)(2,1)S(1)}, u32[]{:S(2)}, u32[]{:S(2)}) collective-permute-start(bf16[165,8]{0,1:T(8,128)(2,1)S(1)} %select_bitcast_fusion.6), channel_id=1, source_target_pairs={{0,2},{1,3},{2,0},{3,1},{4,6},{5,7},{6,4},{7,5},{8,10},{9,11},{10,... | collective-permute-start | bytes 7928 | tf_op jit(solution)/shard_map/ppermute | solution.py:17
  51.4 6.1 %collective-permute-start.4 = (bf16[165,8]{0,1:T(8,128)(2,1)S(1)}, bf16[165,8]{0,1:T(8,128)(2,1)S(1)}, u32[]{:S(2)}, u32[]{:S(2)}) collective-permute-start(bf16[165,8]{0,1:T(8,128)(2,1)S(1)} %select_bitcast_fusion.5), channel_id=1, source_target_pairs={{0,4},{1,5},{2,6},{3,7},{4,0},{5,1},{6,2},{7,3},{8,12},{9,13},{10,... | collective-permute-start | bytes 7928 | tf_op jit(solution)/shard_map/ppermute | solution.py:17
  58.2 7.6 %collective-permute-start.5 = (bf16[165,8]{0,1:T(8,128)(2,1)S(1)}, bf16[165,8]{0,1:T(8,128)(2,1)S(1)}, u32[]{:S(2)}, u32[]{:S(2)}) collective-permute-start(bf16[165,8]{0,1:T(8,128)(2,1)S(1)} %select_bitcast_fusion.4), channel_id=1, source_target_pairs={{0,8},{1,9},{2,10},{3,11},{4,12},{5,13},{6,14},{7,15},{8,0},{9,1},... | collective-permute-start | bytes 7928 | tf_op jit(solution)/shard_map/ppermute | solution.py:17
  66.4 3.6 %collective-permute-start.6 = (bf16[165,8]{0,1:T(8,128)(2,1)S(1)}, bf16[165,8]{0,1:T(8,128)(2,1)S(1)}, u32[]{:S(2)}, u32[]{:S(2)}) collective-permute-start(bf16[165,8]{0,1:T(8,128)(2,1)S(1)} %select_bitcast_fusion.3), channel_id=1, source_target_pairs={{0,16},{16,0},{32,48},{48,32},{1,17},{17,1},{33,49},{49,33},{2,18}... | collective-permute-start | bytes 7928 | tf_op jit(solution)/shard_map/ppermute | solution.py:17
  70.7 48.5 %collective-permute-start.7 = (bf16[165,8]{0,1:T(8,128)(2,1)S(1)}, bf16[165,8]{0,1:T(8,128)(2,1)S(1)}, u32[]{:S(2)}, u32[]{:S(2)}) collective-permute-start(bf16[165,8]{0,1:T(8,128)(2,1)S(1)} %select_bitcast_fusion.2), channel_id=1, source_target_pairs={{0,32},{16,48},{32,0},{48,16},{1,33},{17,49},{33,1},{49,17},{2,34}... | collective-permute-start | bytes 7928 | tf_op jit(solution)/shard_map/ppermute | solution.py:17
  74.3 45.5 %copy-start.13 = (pred[8]{0:T(512)(128)(4,1)S(1)}, pred[8]{0:T(512)(128)(4,1)}, u32[]{:S(2)}) copy-start(pred[8]{0:T(512)(128)(4,1)} %get-tuple-element.137) | copy-start | bytes 28
  74.3 47.1 %copy-start.7 = (f32[2048]{0:T(1024)S(1)}, f32[2048]{0:T(1024)}, u32[]{:S(2)}) copy-start(f32[2048]{0:T(1024)} %copy-done.6) | copy-start | bytes 24580
  74.3 49.7 %copy-start.12 = (pred[8]{0:T(512)(128)(4,1)S(1)}, pred[8]{0:T(512)(128)(4,1)}, u32[]{:S(2)}) copy-start(pred[8]{0:T(512)(128)(4,1)} %get-tuple-element.130) | copy-start | bytes 28
  74.3 53.1 %copy-start.8 = (f32[26]{0:T(128)S(1)}, f32[26]{0:T(128)}, u32[]{:S(2)}) copy-start(f32[26]{0:T(128)} %constant.524) | copy-start | bytes 316
  74.3 53.1 %copy-start.9 = (f32[26]{0:T(128)S(1)}, f32[26]{0:T(128)}, u32[]{:S(2)}) copy-start(f32[26]{0:T(128)} %constant.523) | copy-start | bytes 316
  74.3 53.1 %copy-start.10 = (f32[26]{0:T(128)S(1)}, f32[26]{0:T(128)}, u32[]{:S(2)}) copy-start(f32[26]{0:T(128)} %constant.522) | copy-start | bytes 316
  119.8 3.6 %collective-permute-start.8 = (bf16[165,8]{0,1:T(8,128)(2,1)S(1)}, bf16[165,8]{0,1:T(8,128)(2,1)S(1)}, u32[]{:S(2)}, u32[]{:S(2)}) collective-permute-start(bf16[165,8]{0,1:T(8,128)(2,1)S(1)} %select_bitcast_fusion.1), channel_id=1, source_target_pairs={{0,64},{64,0},{128,192},{192,128},{1,65},{65,1},{129,193},{193,129... | collective-permute-start | bytes 7928 | tf_op jit(solution)/shard_map/ppermute | solution.py:17
  124.1 29.2 %collective-permute-start.9 = (bf16[165,8]{0,1:T(8,128)(2,1)S(1)}, bf16[165,8]{0,1:T(8,128)(2,1)S(1)}, u32[]{:S(2)}, u32[]{:S(2)}) collective-permute-start(bf16[165,8]{0,1:T(8,128)(2,1)S(1)} %select_bitcast_fusion), channel_id=1, source_target_pairs={{0,128},{64,192},{128,0},{192,64},{1,129},{65,193},{129,1},{193,65... | collective-permute-start | bytes 7928 | tf_op jit(solution)/shard_map/ppermute | solution.py:17
  175.4 29.2 %copy-start.1 = (f32[165,2048]{0,1:T(8,128)S(1)}, f32[165,2048]{0,1:T(8,128)}, u32[]{:S(2)}) copy-start(f32[165,2048]{0,1:T(8,128)} %copy-done) | copy-start | bytes 4055044
  175.4 31.0 %copy-start.11 = (s32[32]{0:T(128)S(1)}, s32[32]{0:T(128)}, u32[]{:S(2)}) copy-start(s32[32]{0:T(128)} %param.20) | copy-start | bytes 388
  (1 other events, 0.6 us)
where the time goes:
time: 208 us; the launch traced here: 207 us
  local copies, waits for them, and re-layouts  101 us (49%)
  other arithmetic  36.3 us (17%)
  matrix products  32.1 us (15%)
  starting transfers between devices  25 us (12%)
  waiting for transfers between devices  11.1 us (5%)
    reshape x1, local copies, waits for them, and re-layouts, local(): operators = far_operators.reshape(term_count, list_count, term_count)  44.8 us
    dot_general x1, matrix products, local(): jnp.einsum('klt,tlb->kb', operators, columns, preferred_element_type=jnp....  29.2 us
    gather x1, local copies, waits for them, and re-layouts, local(): jnp.take(held_terms, jnp.clip(far_slots, 0, held_terms.shape[1] - 1), axi...  22.1 us
    ppermute x8, starting transfers between devices, swapped(): lax.ppermute(shard, axis, [(i, i ^ 1 << apart) for i in range(lax.axis_si...  19.4 us
    reduce_sum x2, other arithmetic, near_block(): return jnp.sum(source_q[:, :, None, :] * lax.rsqrt(dist_sq), axis=(0, 3))  13.2 us
    ppermute x8, waiting for transfers between devices, swapped(): lax.ppermute(shard, axis, [(i, i ^ 1 << apart) for i in range(lax.axis_si...  11.1 us
    gather x1, local copies, waits for them, and re-layouts, monomials(): powers[table_np[:, 0], 0] * powers[table_np[:, 1], 1]  5.98 us
    gather x1, local copies, waits for them, and re-layouts, monomials(): powers[table_np[:, 1], 1]  5.75 us
  transfers between devices with their start and end apart: 10, of which 5 were waited for; matrix products, arithmetic and copies ran while one was open for 54% of the time, Pallas kernels for 0%

commit v1 on v0

v1 whole, which is shorter than its diff:
```python
import itertools

import jax
import jax.numpy as jnp
import numpy as np
from jax import lax
from jax.experimental import pallas as pl
from jax.experimental.pallas import tpu as pltpu
from jax.sharding import PartitionSpec as P

ORDER = 8
TERMS = 165
ROWS = 168
LIST = 189
BOXES = 32
SLOTS = 64
ATOMS = BOXES * SLOTS
HALO = 8
EXT = BOXES + 2 * HALO
SOFT2 = 0.0625
GROUP = 16
F32 = jnp.float32
BF16 = jnp.bfloat16
NT = (((1,), (1,)), ((), ()))
MESH = pl.DeviceIdType.MESH
SHIFTS = [s for s in itertools.product((-1, 0, 1), repeat=3) if s != (0, 0, 0)] + [(0, 0, 0)] * 2
PAIRS = len(SHIFTS) // 2


def degree_start(n):
    return n * (n + 1) * (n + 2) // 6


def low(m):
    return (m & -m).bit_length() - 1


def flipped(v, mask, bits):
    for b in range(bits):
        if mask >> b & 1:
            v = v + (1 << b) - (2 << b) * ((v // (1 << b)) % 2)
    return v


def partner(rnd, m):
    if rnd == 0:
        return {"gz": flipped(lax.axis_index("gz"), m, 4)}
    return {
        "gy": flipped(lax.axis_index("gy"), m & 3, 2),
        "gx": flipped(lax.axis_index("gx"), m >> 2, 2),
    }


def iota(shape, dim):
    return lax.broadcasted_iota(jnp.int32, shape, dim)


def fiota(shape, dim):
    return iota(shape, dim).astype(F32)


def split2(v):
    hi = v.astype(BF16)
    return hi, (v - hi.astype(F32)).astype(BF16)


def split3(v):
    hi = v.astype(BF16)
    rest = v - hi.astype(F32)
    mid = rest.astype(BF16)
    return hi, mid, (rest - mid.astype(F32)).astype(BF16)


def dot(a, b, dims=None):
    if dims is None:
        return jnp.dot(a, b, preferred_element_type=F32)
    return lax.dot_general(a, b, dims, preferred_element_type=F32)


def onehot(cond):
    return jnp.where(cond, 1.0, 0.0)


def main_tail_rows(cols, step, width):
    lanes = fiota((8, width), 1)
    rows = []
    for i in range(4):
        at = cols[8 * i : 8 * i + 8]
        rows.append(onehot(lanes == at))
        rows.append(onehot(lanes == at + step))
    return jnp.concatenate(rows, axis=0).astype(BF16)


def routed(tab_rows, tab_cols, base):
    lane = fiota((1, 128), 1)
    lane8 = (iota((1, 128), 1) % 8).astype(F32)
    sub = fiota((32, 1), 0)
    sub8 = (iota((32, 1), 0) % 8).astype(F32)

    def first_row(m):
        s = tab_rows[m : m + 1]
        return jnp.where(s < base, 16.0 * (m - 1) + lane8, 16.0 * m + s - base)

    def first_col(m):
        s = tab_cols[:32, m : m + 1]
        return jnp.where(s < base, 16.0 * (m - 1) + sub8, 16.0 * m + s - base)

    def looked_up(m, table_row, section):
        s = tab_cols[8 * section : 8 * section + 8, m : m + 1]
        lanes = fiota((8, 128), 1)
        found = jnp.sum(jnp.where(lanes == s - base, table_row, 0.0), axis=1, keepdims=True)
        return jnp.where(s < base, 16.0 * (m - 1) + sub8[:8], found)

    table4 = jnp.where(lane < 8, 16.0 * 4 + lane8, first_row(6))
    table12 = jnp.where(sub < 8, 16.0 * 12 + sub8, first_col(14))
    s12 = tab_rows[12:13]
    found12 = jnp.sum(jnp.where(fiota((32, 128), 0) == s12 - base, table12, 0.0), axis=0, keepdims=True)
    row12 = jnp.where(s12 < base, 16.0 * 11 + lane8, found12)
    table8 = jnp.where(lane < 8, 16.0 * 8 + lane8, jnp.where(lane < 16, first_row(10), row12))
    return jnp.concatenate(
        [sub8[:8], first_col(2)[8:16], looked_up(4, table4, 2), looked_up(8, table8, 3)], axis=0
    )


def kernel(
    offs_ref, q_ref, counts_ref, near_ref, far_ref, branch_ref, op_hbm, shift_ref, out_ref,
    opv, tv, p8, dup, tcol, accs, tabrow, tabs, own2, snd1, snd2, rcv1, rcv2, held, oh, col, tail,
    op_sem, tss, trs, hss, hrs, ss1, rs1, ss2, rs2,
):
    op_copy = pltpu.make_async_copy(op_hbm, opv, op_sem)
    op_copy.start()
    gz = lax.axis_index("gz")
    gzs = lax.axis_size("gz")
    barrier = pltpu.get_barrier_semaphore()
    for rnd in range(2):
        for m in range(1, GROUP):
            pl.semaphore_signal(barrier, inc=1, device_id=partner(rnd, m), device_id_type=MESH)

    lo8 = iota((8, 128), 1) < SLOTS
    slot_in_box = iota((1, 128), 1) % SLOTS
    lo1 = iota((1, 128), 1) < SLOTS
    p8[...] = jnp.zeros((8, ATOMS), F32)
    p8[0:3, :] = offs_ref[...]
    for r in range(BOXES // 2):
        count = jnp.where(lo1, counts_ref[2 * r], counts_ref[2 * r + 1])
        span = slice(128 * r, 128 * r + 128)
        p8[3:4, span] = jnp.where(slot_in_box < count, q_ref[:, span], 0.0)
    for r in range(BOXES // 2):
        span = slice(128 * r, 128 * r + 128)
        here = p8[:, span]
        other = pltpu.roll(here, SLOTS, 1)
        dup[HALO + 2 * r] = jnp.where(lo8, here, other)
        dup[HALO + 2 * r + 1] = jnp.where(lo8, other, here)
        tcol[span, :] = jnp.transpose(here)
    dup[EXT] = jnp.zeros((8, 128), F32)

    branch = branch_ref[0].astype(F32).astype(BF16)
    spread = onehot(iota((8, 128), 1) % 8 == iota((8, 128), 0)).astype(BF16)
    wide = dot(branch, spread)
    tabrow[...] = jnp.sum(
        jnp.where(iota((8, 128), 1) // 8 == iota((8, 128), 0), wide, 0.0), axis=0, keepdims=True
    )
    stretch = onehot(iota((64, 8), 0) // 8 == iota((64, 8), 1)).astype(BF16)
    tall = dot(stretch, branch)
    scol = jnp.sum(jnp.where(iota((64, 8), 1) == iota((64, 8), 0) % 8, tall, 0.0), axis=1, keepdims=True)

    def terms_block(blk, _):
        span = pl.ds(pl.multiple_of(blk * 256, 256), 256)
        x, y, z = (2.0 * p8[c : c + 1, span] for c in range(3))
        tv[0:1, span] = jnp.ones((1, 256), F32)
        for n in range(1, ORDER + 1):
            before, here, kept = degree_start(n - 1), degree_start(n), n * (n + 1) // 2
            tv[here : here + kept, span] = tv[before : before + kept, span] * x
            tv[here + kept : here + kept + n, span] = tv[before + kept - n : before + kept, span] * y
            tv[here + kept + n : here + kept + n + 1, span] = tv[before + kept - 1 : before + kept, span] * z
        tv[TERMS:ROWS, span] = jnp.zeros((ROWS - TERMS, 256), F32)
        return 0

    lax.fori_loop(0, ATOMS // 256, terms_block, 0)

    pl.semaphore_wait(barrier, 2 * (GROUP - 1))
    sends = []
    table_copies = []
    for rnd in range(2):
        for m in range(1, GROUP):
            at = rnd * GROUP + m
            c = pltpu.make_async_remote_copy(
                src_ref=tabrow, dst_ref=tabs.at[at], send_sem=tss.at[at], recv_sem=trs.at[at],
                device_id=partner(rnd, m), device_id_type=MESH,
            )
            c.start()
            table_copies.append(c)
    up = pltpu.make_async_remote_copy(
        src_ref=dup.at[pl.ds(BOXES, HALO)], dst_ref=dup.at[pl.ds(0, HALO)],
        send_sem=hss.at[0], recv_sem=hrs.at[0], device_id={"gz": (gz + 1) % gzs}, device_id_type=MESH,
    )
    down = pltpu.make_async_remote_copy(
        src_ref=dup.at[pl.ds(HALO, HALO)], dst_ref=dup.at[pl.ds(BOXES + HALO, HALO)],
        send_sem=hss.at[1], recv_sem=hrs.at[1], device_id={"gz": (gz + gzs - 1) % gzs}, device_id_type=MESH,
    )
    up.start()
    down.start()

    head = jnp.zeros((64, ROWS), F32)
    rest = jnp.zeros((32, ROWS), F32)
    for blk in range(ATOMS // 256):
        span = slice(256 * blk, 256 * blk + 256)
        mine = (256 * blk + iota((BOXES, 256), 1)) // SLOTS == iota((BOXES, 256), 0)
        qh, qm = split2(jnp.where(mine, p8[3:4, span], 0.0))
        th, tm = split2(tv[:, span])
        head = head + dot(jnp.concatenate([qh, qm], axis=0), th, NT)
        rest = rest + dot(qh, tm, NT)
    multipoles = head[:32] + head[32:] + rest
    tail[...] = jnp.zeros((32, 128), F32)
    tail[:, 0 : ROWS - 128] = multipoles[:, 128:ROWS]
    own_main = multipoles[:, 0:128].astype(BF16)
    own_tail = tail[...].astype(BF16)
    own2[0:32] = own_main
    own2[32:64] = own_tail
    held[0:32, 0:128] = own_main
    held[0:32, 128:256] = own_tail

    picked1 = jnp.where(scol[:32] < 32, scol[:32], -1000.0)
    snd1[...] = dot(main_tail_rows(picked1, 32.0, 64), own2[...]).astype(BF16).reshape(4, 16, 128)

    def exchange(rnd, snd, rcv, ss, rs):
        out = []
        for m in range(1, GROUP):
            c = pltpu.make_async_remote_copy(
                src_ref=snd.at[low(m)], dst_ref=rcv.at[m - 1], send_sem=ss.at[m - 1], recv_sem=rs.at[m - 1],
                device_id=partner(rnd, m), device_id_type=MESH,
            )
            c.start()
            out.append(c)
        return out

    round1 = exchange(0, snd1, rcv1, ss1, rs1)

    for c in table_copies:
        c.wait_recv()
    tabs[0] = tabrow[...]
    tabs[GROUP] = tabrow[...]
    rows1 = jnp.concatenate([tabs[m] for m in range(GROUP)], axis=0)
    rows2 = jnp.concatenate([tabs[GROUP + m] for m in range(GROUP)], axis=0)
    cols1 = jnp.transpose(jnp.concatenate([rows1, rows2] + [jnp.zeros((96, 128), F32)], axis=0))
    from1 = routed(rows1, cols1[0:32, 0:16], 32.0)
    from2 = routed(pltpu.roll(rows2, 96, 1), cols1[32:64, 16:32], 64.0)
    own_late = scol[32:64]
    fwd = onehot(fiota((32, 32), 1) == own_late - 32.0).astype(BF16)
    via = dot(fwd, jnp.broadcast_to(from1, (32, 128)).astype(BF16))[:, 0:1]
    late = jnp.where(jnp.logical_and(own_late >= 32, own_late < 64), via, -1000.0)
    lanes240 = fiota((32, 240), 1)
    select1 = jnp.concatenate(
        [
            main_tail_rows(late, 8.0, 240),
            onehot(lanes240 == from1).astype(BF16),
            onehot(lanes240 == from1 + 8.0).astype(BF16),
        ],
        axis=0,
    )
    select2 = jnp.concatenate(
        [onehot(lanes240 == from2).astype(BF16), onehot(lanes240 == from2 + 8.0).astype(BF16)], axis=0
    )
    picked2 = jnp.where(own_late < 32, own_late, -1000.0)
    from_own = dot(main_tail_rows(picked2, 32.0, 64), own2[...])

    up.wait_recv()
    down.wait_recv()
    base_box = (
        (lax.axis_index("gx") * lax.axis_size("gy") + lax.axis_index("gy")) * gzs + gz
    ) * BOXES - HALO

    def near_box(g, _):
        lo = iota((8, 128), 1) < SLOTS
        at = pl.ds(pl.multiple_of(g * SLOTS, SLOTS), SLOTS)
        targets = tcol[at, :]
        t = [
            [jnp.broadcast_to(targets[8 * k : 8 * k + 8, c : c + 1], (8, 128)) for k in range(8)]
            for c in range(3)
        ]
        acc = [jnp.zeros((8, 128), F32) for _ in range(8)]
        for p in range(PAIRS):
            if p < PAIRS - 1:
                first, second = near_ref[2 * p, g], near_ref[2 * p + 1, g]
                first = jnp.where(first < 0, EXT, jnp.clip(first - base_box, 0, EXT - 1))
                second = jnp.where(second < 0, EXT, jnp.clip(second - base_box, 0, EXT - 1))
                src = jnp.where(lo, dup[first], dup[second]) + shift_ref[p]
            else:
                src = jnp.where(lo, dup[g + HALO], 0.0)
            sx, sy, sz, sq = (jnp.broadcast_to(src[c : c + 1], (8, 128)) for c in range(4))
            for k in range(8):
                dx, dy, dz = sx - t[0][k], sy - t[1][k], sz - t[2][k]
                weight = sq
                if p == PAIRS - 1:
                    weight = jnp.where(iota((8, 128), 1) == 8 * k + iota((8, 128), 0), 0.0, sq)
                acc[k] = acc[k] + weight * lax.rsqrt(dx * dx + (dy * dy + (dz * dz + SOFT2)))
        accs[at, :] = jnp.concatenate(acc, axis=0)
        return 0

    lax.fori_loop(0, BOXES // 2, near_box, 0)

    for c in round1:
        c.wait_recv()
    got = dot(select1, rcv1[...].reshape(240, 128))
    snd2[...] = (got[0:64] + from_own).astype(BF16).reshape(4, 16, 128)
    round2 = exchange(1, snd2, rcv2, ss2, rs2)
    held[32:64, 0:128] = got[64:96].astype(BF16)
    held[32:64, 128:256] = got[96:128].astype(BF16)

    far_cols = jnp.transpose(
        jnp.concatenate(
            [
                jnp.concatenate([far_ref[...].astype(F32), jnp.zeros((256 - LIST, BOXES), F32)], axis=0),
                jnp.zeros((256, 96), F32),
            ],
            axis=1,
        )
    )
    lanes96 = fiota((BOXES, 96), 1)
    for l in range(LIST):
        oh[BOXES * l : BOXES * l + BOXES, :] = onehot(lanes96 == far_cols[0:BOXES, l : l + 1]).astype(BF16)
    lax.fori_loop(BOXES // 2, BOXES, near_box, 0)
    ah, am = split2(accs[...])
    ones = jnp.ones((8, 128), BF16)
    near_row = (dot(ones, ah, NT) + dot(ones, am, NT))[0:1]

    for c in round2:
        c.wait_recv()
    got2 = dot(select2, rcv2[...].reshape(240, 128))
    held[64:96, 0:128] = got2[0:32].astype(BF16)
    held[64:96, 128:256] = got2[32:64].astype(BF16)

    table = held[...]

    lane32 = iota((BOXES, 128), 1)

    def gather(grp, carry):
        span = pl.ds(pl.multiple_of(grp * (7 * BOXES), 7 * BOXES), 7 * BOXES)
        seven = dot(oh[span, :], table)
        for i in range(7):
            pos = (grp * 7 + i) * TERMS
            r = pos % 128
            tile = pos // 128
            piece = seven[BOXES * i : BOXES * i + BOXES]
            a = pltpu.roll(piece[:, 0:128], r, 1)
            b = pltpu.roll(piece[:, 128:256], r, 1)
            before = lane32 < r
            one = jnp.where(before, carry, a)
            two = jnp.where(before, a, b)
            col[:, pl.ds(pl.multiple_of(tile * 128, 128), 128)] = one.astype(BF16)
            col[:, pl.ds(pl.multiple_of(tile * 128 + 128, 128), 128)] = two.astype(BF16)
            carry = jnp.where(r + TERMS >= 256, b, two)
        return carry

    last = lax.fori_loop(0, LIST // 7, gather, jnp.zeros((BOXES, 128), F32))
    op_copy.wait()
    local = dot(opv[...], col[:, 0 : LIST * TERMS], NT)

    l1, l2, l3 = split3(local)
    parts = jnp.concatenate([l1.astype(F32), l2.astype(F32), l3.astype(F32)], axis=1).astype(BF16)
    for blk in range(ATOMS // 256):
        span = slice(256 * blk, 256 * blk + 256)
        boxes = onehot((256 * blk + iota((96, 256), 1)) // SLOTS == iota((96, 256), 0) % BOXES).astype(BF16)
        there = dot(parts, boxes)
        far = jnp.sum(there * tv[0:TERMS, span], axis=0, keepdims=True)
        both = far + near_row[:, span]
        for h in range(2):
            r = 2 * blk + h
            count = jnp.where(lo1, counts_ref[2 * r], counts_ref[2 * r + 1])
            out_ref[:, 128 * r : 128 * r + 128] = jnp.where(
                slot_in_box < count, both[:, 128 * h : 128 * h + 128], 0.0
            )
    for c in table_copies + round1 + round2 + [up, down]:
        c.wait_send()


def shift_tiles():
    tiles = np.zeros((PAIRS, 8, 128), np.float32)
    for p in range(PAIRS):
        for c in range(3):
            tiles[p, c, :SLOTS] = SHIFTS[2 * p][c]
            tiles[p, c, SLOTS:] = SHIFTS[2 * p + 1][c]
    return tiles


def local_part(leaf_offsets, latent_charges, atom_counts, near_boxes, far_slots, branch_slots, far_operators):
    vmem = pl.BlockSpec(memory_space=pltpu.VMEM)
    smem = pl.BlockSpec(memory_space=pltpu.SMEM)
    sem = pltpu.SemaphoreType.DMA
    out = pl.pallas_call(
        kernel,
        out_shape=jax.ShapeDtypeStruct((1, ATOMS), F32),
        in_specs=[vmem, vmem, smem, smem, vmem, vmem, pl.BlockSpec(memory_space=pl.ANY), vmem],
        out_specs=vmem,
        scratch_shapes=[
            pltpu.VMEM((TERMS, LIST * TERMS), BF16),
            pltpu.VMEM((ROWS, ATOMS), F32),
            pltpu.VMEM((8, ATOMS), F32),
            pltpu.VMEM((EXT + 1, 8, 128), F32),
            pltpu.VMEM((ATOMS, 8), F32),
            pltpu.VMEM((ATOMS, 128), F32),
            pltpu.VMEM((1, 128), F32),
            pltpu.VMEM((2 * GROUP, 1, 128), F32),
            pltpu.VMEM((64, 128), BF16),
            pltpu.VMEM((4, 16, 128), BF16),
            pltpu.VMEM((4, 16, 128), BF16),
            pltpu.VMEM((GROUP - 1, 16, 128), BF16),
            pltpu.VMEM((GROUP - 1, 16, 128), BF16),
            pltpu.VMEM((96, 256), BF16),
            pltpu.VMEM((LIST * BOXES, 96), BF16),
            pltpu.VMEM((BOXES, 31360), BF16),
            pltpu.VMEM((BOXES, 128), F32),
            sem,
            sem((2 * GROUP,)),
            sem((2 * GROUP,)),
            sem((2,)),
            sem((2,)),
            sem((GROUP - 1,)),
            sem((GROUP - 1,)),
            sem((GROUP - 1,)),
            sem((GROUP - 1,)),
        ],
        compiler_params=pltpu.CompilerParams(
            collective_id=0, has_side_effects=True, vmem_limit_bytes=56 << 20
        ),
    )(
        leaf_offsets,
        latent_charges.reshape(1, ATOMS),
        atom_counts,
        near_boxes,
        far_slots,
        branch_slots,
        far_operators,
        shift_tiles(),
    )
    return out.reshape(-1)


def solution(mesh):
    boxes = ("gx", "gy", "gz")
    in_specs = (P(None, boxes), P(boxes), P(boxes), P(None, boxes), P(None, boxes), P(boxes, None, None), P())
    return jax.shard_map(local_part, mesh=mesh, in_specs=in_specs, out_specs=P(boxes), check_vma=False)
```

time: 208 us -> 43.6 us (0.21)
  the two profiles are of different devices: /device:TPU:32 before, /device:TPU:1 now
where the time goes in v1:
time: 43.6 us; the launch traced here: 43.4 us
  Pallas kernels  40.6 us (93%)
  local copies, waits for them, and re-layouts  2.77 us (6%)
    pallas_call x1, Pallas kernels, local_part(): pl.pallas_call(kernel, out_shape=jax.ShapeDtypeStruct((1, ATOMS), F32), i...  40.6 us
    unnamed x2, local copies, waits for them, and re-layouts  2.77 us

profile of v1, /device:TPU:1, one launch (start us, length us, event | category | flops | bytes accessed | tf_op | source)
XLA Modules:
  0.0 43.4 jit_solution(8568861958255518495)
XLA Ops:
  0.0 1.5 %copy.9.far_ref = s32[189,32]{1,0:T(8,128)} copy(s32[189,32]{0,1:T(8,128)} %param.12) | data formatting | bytes 48384 | tf_op args[4]
  1.5 40.6 %shard_map.82 = f32[1,2048]{1,0:T(1,128)} custom-call(f32[3,2048]{1,0:T(4,128)} %offs_ref.1, f32[1,2048]{1,0:T(1,128)} %bitcast.3, s32[32]{0:T(128)} %counts_ref.1, s32[26,32]{1,0:T(8,128)} %near_ref.1, s32[189,32]{1,0:T(8,128)} %copy.9.far_ref, s32[1,8,8]{2,1,0:T(8,128)} %branch_ref.1, bf16[165,31185]{1,0:T(8,128)(2,1)} %op_hbm.1, ...), custom_call_target="tpu_custom_call" | custom-call | tf_op jit(solution)/shard_map/pallas_call | solution.py:390
  42.1 1.3 %copy.11 = f32[2048]{0:T(1024)} copy(f32[2048]{0:T(1024)} %bitcast.2) | data formatting | bytes 16384

commit v2 on v1

--- a/solution.py
+++ b/solution.py
@@ -122,9 +122,51 @@
     )
 
 
+def stacked(*cases):
+    row = iota((8, 128), 0)
+    tiles = [
+        jnp.where(row < 3, first, jnp.where(row == 3, third, jnp.where(row == 4, fourth, last)))
+        for first, third, fourth, last in cases
+    ]
+    return jnp.concatenate(tiles, axis=0)
+
+
+def norm_row(tile):
+    square = tile * tile
+    return square[0:1] + square[1:2] + square[2:3]
+
+
+def target_rows(tile):
+    row = iota((8, 128), 0)
+    both = jnp.where(row == 4, norm_row(tile), jnp.where(row < 3, tile, pltpu.roll(tile, 5, 0)))
+    u1, u2, u3 = (part.astype(F32) for part in split3(both))
+    return stacked(
+        (-2.0 * u1, 1.0, u1, 2.0),
+        (-2.0 * u2, 0.0, u2, -2.0 * u1),
+        (-2.0 * u3, 0.0, u3, -2.0 * u2),
+        (-2.0 * u1, 1.0, 1.0, 2.0),
+        (-2.0 * u2, 0.0, 0.0, -2.0 * u3),
+        (-2.0 * u1, 1.0, 0.0, 2.0),
+    )
+
+
+def source_rows(tile):
+    row = iota((8, 128), 0)
+    both = jnp.where(row == 3, norm_row(tile) + SOFT2, jnp.where(row < 3, tile, pltpu.roll(tile, 5, 0)))
+    s1, s2, s3 = (part.astype(F32) for part in split3(both))
+    return stacked(
+        (s1, s1, 1.0, s1),
+        (s1, 0.0, 1.0, 1.0),
+        (s1, 0.0, 1.0, 1.0),
+        (s2, s2, 1.0, s2),
+        (s2, 0.0, 0.0, 1.0),
+        (s3, s3, 0.0, s3),
+    )
+
+
 def kernel(
-    offs_ref, q_ref, counts_ref, near_ref, far_ref, branch_ref, op_hbm, shift_ref, out_ref,
-    opv, tv, p8, dup, tcol, accs, tabrow, tabs, own2, snd1, snd2, rcv1, rcv2, held, oh, col, tail,
+    offs_ref, q_ref, counts_ref, near_ref, far_ref, branch_ref, op_hbm, factor_ref, out_ref,
+    opv, tv, p8, dup, aims, sources, charges, accs, tabrow, tabs, own2, snd1, snd2, rcv1, rcv2, held, oh, col, tail,
     op_sem, tss, trs, hss, hrs, ss1, rs1, ss2, rs2,
 ):
     op_copy = pltpu.make_async_copy(op_hbm, opv, op_sem)
@@ -151,7 +193,7 @@
         other = pltpu.roll(here, SLOTS, 1)
         dup[HALO + 2 * r] = jnp.where(lo8, here, other)
         dup[HALO + 2 * r + 1] = jnp.where(lo8, other, here)
-        tcol[span, :] = jnp.transpose(here)
+        aims[span, :] = jnp.transpose(target_rows(here)).astype(BF16)
     dup[EXT] = jnp.zeros((8, 128), F32)
 
     branch = branch_ref[0].astype(F32).astype(BF16)
@@ -270,34 +312,39 @@
         (lax.axis_index("gx") * lax.axis_size("gy") + lax.axis_index("gy")) * gzs + gz
     ) * BOXES - HALO
 
+    for e in range(EXT + 1):
+        tile = dup[e]
+        sources[e] = source_rows(tile).astype(BF16)
+        charges[e] = jnp.broadcast_to(tile[3:4], (8, 128))
+
     def near_box(g, _):
         lo = iota((8, 128), 1) < SLOTS
+        lo48 = iota((48, 128), 1) < SLOTS
         at = pl.ds(pl.multiple_of(g * SLOTS, SLOTS), SLOTS)
-        targets = tcol[at, :]
-        t = [
-            [jnp.broadcast_to(targets[8 * k : 8 * k + 8, c : c + 1], (8, 128)) for k in range(8)]
-            for c in range(3)
-        ]
+        aim = aims[at, :]
         acc = [jnp.zeros((8, 128), F32) for _ in range(8)]
-        for p in range(PAIRS):
-            if p < PAIRS - 1:
-                first, second = near_ref[2 * p, g], near_ref[2 * p + 1, g]
-                first = jnp.where(first < 0, EXT, jnp.clip(first - base_box, 0, EXT - 1))
-                second = jnp.where(second < 0, EXT, jnp.clip(second - base_box, 0, EXT - 1))
-                src = jnp.where(lo, dup[first], dup[second]) + shift_ref[p]
-            else:
-                src = jnp.where(lo, dup[g + HALO], 0.0)
-            sx, sy, sz, sq = (jnp.broadcast_to(src[c : c + 1], (8, 128)) for c in range(4))
-            for k in range(8):
-                dx, dy, dz = sx - t[0][k], sy - t[1][k], sz - t[2][k]
-                weight = sq
-                if p == PAIRS - 1:
-                    weight = jnp.where(iota((8, 128), 1) == 8 * k + iota((8, 128), 0), 0.0, sq)
-                acc[k] = acc[k] + weight * lax.rsqrt(dx * dx + (dy * dy + (dz * dz + SOFT2)))
+        for p0 in range(0, PAIRS, 2):
+            there, weight = [], []
+            for p in (p0, p0 + 1):
+                if p < PAIRS - 1:
+                    first, second = near_ref[2 * p, g], near_ref[2 * p + 1, g]
+                    first = jnp.where(first < 0, EXT, jnp.clip(first - base_box, 0, EXT - 1))
+                    second = jnp.where(second < 0, EXT, jnp.clip(second - base_box, 0, EXT - 1))
+                else:
+                    first, second = g + HALO, EXT
+                there.append(jnp.where(lo48, sources[first], sources[second]) * factor_ref[p])
+                weight.append(jnp.where(lo, charges[first], charges[second]))
+            dist = dot(aim, jnp.concatenate(there, axis=1))
+            for i in range(2):
+                for k in range(8):
+                    w = weight[i]
+                    if p0 + i == PAIRS - 1:
+                        w = jnp.where(iota((8, 128), 1) == 8 * k + iota((8, 128), 0), 0.0, w)
+                    acc[k] = acc[k] + w * lax.rsqrt(dist[8 * k : 8 * k + 8, 128 * i : 128 * i + 128])
         accs[at, :] = jnp.concatenate(acc, axis=0)
         return 0
 
-    lax.fori_loop(0, BOXES // 2, near_box, 0)
+    lax.fori_loop(0, BOXES // 2, near_box, 0, unroll=8)
 
     for c in round1:
         c.wait_recv()
@@ -307,19 +354,11 @@
     held[32:64, 0:128] = got[64:96].astype(BF16)
     held[32:64, 128:256] = got[96:128].astype(BF16)
 
-    far_cols = jnp.transpose(
-        jnp.concatenate(
-            [
-                jnp.concatenate([far_ref[...].astype(F32), jnp.zeros((256 - LIST, BOXES), F32)], axis=0),
-                jnp.zeros((256, 96), F32),
-            ],
-            axis=1,
-        )
-    )
+    far_cols = far_ref[...].astype(F32)
     lanes96 = fiota((BOXES, 96), 1)
     for l in range(LIST):
         oh[BOXES * l : BOXES * l + BOXES, :] = onehot(lanes96 == far_cols[0:BOXES, l : l + 1]).astype(BF16)
-    lax.fori_loop(BOXES // 2, BOXES, near_box, 0)
+    lax.fori_loop(BOXES // 2, BOXES, near_box, 0, unroll=8)
     ah, am = split2(accs[...])
     ones = jnp.ones((8, 128), BF16)
     near_row = (dot(ones, ah, NT) + dot(ones, am, NT))[0:1]
@@ -332,27 +371,12 @@
 
     table = held[...]
 
-    lane32 = iota((BOXES, 128), 1)
-
-    def gather(grp, carry):
-        span = pl.ds(pl.multiple_of(grp * (7 * BOXES), 7 * BOXES), 7 * BOXES)
-        seven = dot(oh[span, :], table)
-        for i in range(7):
-            pos = (grp * 7 + i) * TERMS
-            r = pos % 128
-            tile = pos // 128
-            piece = seven[BOXES * i : BOXES * i + BOXES]
-            a = pltpu.roll(piece[:, 0:128], r, 1)
-            b = pltpu.roll(piece[:, 128:256], r, 1)
-            before = lane32 < r
-            one = jnp.where(before, carry, a)
-            two = jnp.where(before, a, b)
-            col[:, pl.ds(pl.multiple_of(tile * 128, 128), 128)] = one.astype(BF16)
-            col[:, pl.ds(pl.multiple_of(tile * 128 + 128, 128), 128)] = two.astype(BF16)
-            carry = jnp.where(r + TERMS >= 256, b, two)
-        return carry
-
-    last = lax.fori_loop(0, LIST // 7, gather, jnp.zeros((BOXES, 128), F32))
+    for first in range(0, LIST, 8):
+        count = min(8, LIST - first)
+        some = dot(oh[BOXES * first : BOXES * (first + count), :], table).astype(BF16)
+        for i in range(count):
+            pos = (first + i) * TERMS
+            col[:, pos : pos + TERMS] = some[BOXES * i : BOXES * i + BOXES, 0:TERMS]
     op_copy.wait()
     local = dot(opv[...], col[:, 0 : LIST * TERMS], NT)
 
@@ -374,13 +398,16 @@
         c.wait_send()
 
 
-def shift_tiles():
-    tiles = np.zeros((PAIRS, 8, 128), np.float32)
+def factor_tiles():
+    tiles = np.ones((PAIRS, 6, 8, 128), np.float32)
     for p in range(PAIRS):
-        for c in range(3):
-            tiles[p, c, :SLOTS] = SHIFTS[2 * p][c]
-            tiles[p, c, SLOTS:] = SHIFTS[2 * p + 1][c]
-    return tiles
+        for half in range(2):
+            shift = SHIFTS[2 * p + half]
+            lanes = slice(SLOTS * half, SLOTS * half + SLOTS)
+            for c in range(3):
+                tiles[p, :, 5 + c, lanes] = shift[c]
+            tiles[p, 3, 4, lanes] = sum(c * c for c in shift)
+    return tiles.reshape(PAIRS, 48, 128).astype(BF16)
 
 
 def local_part(leaf_offsets, latent_charges, atom_counts, near_boxes, far_slots, branch_slots, far_operators):
@@ -397,7 +424,9 @@
             pltpu.VMEM((ROWS, ATOMS), F32),
             pltpu.VMEM((8, ATOMS), F32),
             pltpu.VMEM((EXT + 1, 8, 128), F32),
-            pltpu.VMEM((ATOMS, 8), F32),
+            pltpu.VMEM((ATOMS, 48), BF16),
+            pltpu.VMEM((EXT + 1, 48, 128), BF16),
+            pltpu.VMEM((EXT + 1, 8, 128), F32),
             pltpu.VMEM((ATOMS, 128), F32),
             pltpu.VMEM((1, 128), F32),
             pltpu.VMEM((2 * GROUP, 1, 128), F32),
@@ -408,7 +437,7 @@
             pltpu.VMEM((GROUP - 1, 16, 128), BF16),
             pltpu.VMEM((96, 256), BF16),
             pltpu.VMEM((LIST * BOXES, 96), BF16),
-            pltpu.VMEM((BOXES, 31360), BF16),
+            pltpu.VMEM((BOXES, 31232), BF16),
             pltpu.VMEM((BOXES, 128), F32),
             sem,
             sem((2 * GROUP,)),
@@ -428,10 +457,10 @@
         latent_charges.reshape(1, ATOMS),
         atom_counts,
         near_boxes,
-        far_slots,
+        far_slots.T,
         branch_slots,
         far_operators,
-        shift_tiles(),
+        factor_tiles(),
     )
     return out.reshape(-1)
 

time: 43.6 us -> 34.3 us (0.79)
  Pallas kernels: 40.6 us -> 32.8 us
  local copies, waits for them, and re-layouts: 2.77 us -> 1.3 us
    pallas_call x1, Pallas kernels: 40.6 us -> 32.8 us  [local_part(): pl.pallas_call(kernel, out_shape=jax.ShapeDtypeStruct((1, ATOMS), F32), i...]
    unnamed x2 -> x1, local copies, waits for them, and re-layouts: 2.77 us -> 1.3 us
where the time goes in v2:
time: 34.3 us; the launch traced here: 34.1 us
  Pallas kernels  32.8 us (96%)
  local copies, waits for them, and re-layouts  1.3 us (4%)
    pallas_call x1, Pallas kernels, local_part(): pl.pallas_call(kernel, out_shape=jax.ShapeDtypeStruct((1, ATOMS), F32), i...  32.8 us
    unnamed x1, local copies, waits for them, and re-layouts  1.3 us

profile of v2, /device:TPU:1, one launch (start us, length us, event | category | flops | bytes accessed | tf_op | source)
XLA Modules:
  0.0 34.1 jit_solution(930248808475869408)
XLA Ops:
  0.0 32.8 %shard_map.82 = f32[1,2048]{1,0:T(1,128)} custom-call(f32[3,2048]{1,0:T(4,128)} %offs_ref.1, f32[1,2048]{1,0:T(1,128)} %bitcast.5, s32[32]{0:T(128)} %counts_ref.1, s32[26,32]{1,0:T(8,128)} %near_ref.1, s32[32,189]{1,0:T(8,128)} %bitcast.3, s32[1,8,8]{2,1,0:T(8,128)} %branch_ref.1, bf16[165,31185]{1,0:T(8,128)(2,1)} %op_hbm.1, ...), custom_call_target="tpu_custom_call" | custom-call | tf_op jit(solution)/shard_map/pallas_call | solution.py:417
  32.8 1.3 %copy.10 = f32[2048]{0:T(1024)} copy(f32[2048]{0:T(1024)} %bitcast.4) | data formatting | bytes 16384

commit v3 on v2

--- a/solution.py
+++ b/solution.py
@@ -91,35 +91,43 @@
     return jnp.concatenate(rows, axis=0).astype(BF16)
 
 
-def routed(tab_rows, tab_cols, base):
+def routed(got, rnd):
+    base = 32.0 * (rnd + 1)
     lane = fiota((1, 128), 1)
     lane8 = (iota((1, 128), 1) % 8).astype(F32)
-    sub = fiota((32, 1), 0)
-    sub8 = (iota((32, 1), 0) % 8).astype(F32)
+    sub8 = fiota((8, 1), 0)
+
+    def named(m):
+        return got[m - 1].astype(F32)[8:16]
+
+    def as_row(m):
+        return pltpu.roll(named(m), 32, 1)[0:1]
+
+    def as_col(m, section):
+        at = 64 + 4 * rnd + section
+        return named(m)[:, at : at + 1]
 
     def first_row(m):
-        s = tab_rows[m : m + 1]
+        s = as_row(m)
         return jnp.where(s < base, 16.0 * (m - 1) + lane8, 16.0 * m + s - base)
 
     def first_col(m):
-        s = tab_cols[:32, m : m + 1]
+        s = as_col(m, 1)
         return jnp.where(s < base, 16.0 * (m - 1) + sub8, 16.0 * m + s - base)
 
     def looked_up(m, table_row, section):
-        s = tab_cols[8 * section : 8 * section + 8, m : m + 1]
-        lanes = fiota((8, 128), 1)
-        found = jnp.sum(jnp.where(lanes == s - base, table_row, 0.0), axis=1, keepdims=True)
-        return jnp.where(s < base, 16.0 * (m - 1) + sub8[:8], found)
+        s = as_col(m, section)
+        found = jnp.sum(jnp.where(fiota((8, 128), 1) == s - base, table_row, 0.0), axis=1, keepdims=True)
+        return jnp.where(s < base, 16.0 * (m - 1) + sub8, found)
 
     table4 = jnp.where(lane < 8, 16.0 * 4 + lane8, first_row(6))
-    table12 = jnp.where(sub < 8, 16.0 * 12 + sub8, first_col(14))
-    s12 = tab_rows[12:13]
-    found12 = jnp.sum(jnp.where(fiota((32, 128), 0) == s12 - base, table12, 0.0), axis=0, keepdims=True)
-    row12 = jnp.where(s12 < base, 16.0 * 11 + lane8, found12)
+    s12 = as_row(12)
+    at12 = s12 - base
+    found12 = jnp.sum(jnp.where(fiota((8, 128), 0) == at12 - 8.0, first_col(14), 0.0), axis=0, keepdims=True)
+    found12 = jnp.where(at12 < 8, 16.0 * 12 + at12, found12)
+    row12 = jnp.where(at12 < 0, 16.0 * 11 + lane8, found12)
     table8 = jnp.where(lane < 8, 16.0 * 8 + lane8, jnp.where(lane < 16, first_row(10), row12))
-    return jnp.concatenate(
-        [sub8[:8], first_col(2)[8:16], looked_up(4, table4, 2), looked_up(8, table8, 3)], axis=0
-    )
+    return jnp.concatenate([sub8, first_col(2), looked_up(4, table4, 2), looked_up(8, table8, 3)], axis=0)
 
 
 def stacked(*cases):
@@ -165,10 +173,16 @@
 
 
 def kernel(
-    offs_ref, q_ref, counts_ref, near_ref, far_ref, branch_ref, op_hbm, factor_ref, out_ref,
-    opv, tv, p8, dup, aims, sources, charges, accs, tabrow, tabs, own2, snd1, snd2, rcv1, rcv2, held, oh, col, tail,
-    op_sem, tss, trs, hss, hrs, ss1, rs1, ss2, rs2,
+    offs_ref, q_ref, counts_ref, near_hbm, far_hbm, branch_ref, op_hbm, factor_hbm, out_ref,
+    opv, tv, p8, dup, aims, sources, charges, accs, near_ref, far_ref, factor_ref, own2, snd1, snd2, rcv1, rcv2, held, oh, col, tail,
+    op_sem, in_sems, hss, hrs, ss1, rs1, ss2, rs2,
 ):
+    loads = [
+        pltpu.make_async_copy(src, dst, in_sems.at[i])
+        for i, (src, dst) in enumerate(((far_hbm, far_ref), (near_hbm, near_ref), (factor_hbm, factor_ref)))
+    ]
+    for c in loads:
+        c.start()
     op_copy = pltpu.make_async_copy(op_hbm, opv, op_sem)
     op_copy.start()
     gz = lax.axis_index("gz")
@@ -199,12 +213,20 @@
     branch = branch_ref[0].astype(F32).astype(BF16)
     spread = onehot(iota((8, 128), 1) % 8 == iota((8, 128), 0)).astype(BF16)
     wide = dot(branch, spread)
-    tabrow[...] = jnp.sum(
+    own_row = jnp.sum(
         jnp.where(iota((8, 128), 1) // 8 == iota((8, 128), 0), wide, 0.0), axis=0, keepdims=True
     )
     stretch = onehot(iota((64, 8), 0) // 8 == iota((64, 8), 1)).astype(BF16)
     tall = dot(stretch, branch)
     scol = jnp.sum(jnp.where(iota((64, 8), 1) == iota((64, 8), 0) % 8, tall, 0.0), axis=1, keepdims=True)
+
+    def named_tile(rnd):
+        lanes = iota((8, 128), 1)
+        tile = jnp.where(lanes >= 96, pltpu.roll(jnp.broadcast_to(own_row, (8, 128)), 96 - 32 * rnd, 1), 0.0)
+        for i in range(4 * rnd, 4 * rnd + 4):
+            tile = jnp.where(lanes == 64 + i, scol[8 * i : 8 * i + 8], tile)
+        none = jnp.zeros((8, 128), F32)
+        return jnp.concatenate([none, tile] * 4, axis=0)
 
     def terms_block(blk, _):
         span = pl.ds(pl.multiple_of(blk * 256, 256), 256)
@@ -219,29 +241,6 @@
         return 0
 
     lax.fori_loop(0, ATOMS // 256, terms_block, 0)
-
-    pl.semaphore_wait(barrier, 2 * (GROUP - 1))
-    sends = []
-    table_copies = []
-    for rnd in range(2):
-        for m in range(1, GROUP):
-            at = rnd * GROUP + m
-            c = pltpu.make_async_remote_copy(
-                src_ref=tabrow, dst_ref=tabs.at[at], send_sem=tss.at[at], recv_sem=trs.at[at],
-                device_id=partner(rnd, m), device_id_type=MESH,
-            )
-            c.start()
-            table_copies.append(c)
-    up = pltpu.make_async_remote_copy(
-        src_ref=dup.at[pl.ds(BOXES, HALO)], dst_ref=dup.at[pl.ds(0, HALO)],
-        send_sem=hss.at[0], recv_sem=hrs.at[0], device_id={"gz": (gz + 1) % gzs}, device_id_type=MESH,
-    )
-    down = pltpu.make_async_remote_copy(
-        src_ref=dup.at[pl.ds(HALO, HALO)], dst_ref=dup.at[pl.ds(BOXES + HALO, HALO)],
-        send_sem=hss.at[1], recv_sem=hrs.at[1], device_id={"gz": (gz + gzs - 1) % gzs}, device_id_type=MESH,
-    )
-    up.start()
-    down.start()
 
     head = jnp.zeros((64, ROWS), F32)
     rest = jnp.zeros((32, ROWS), F32)
@@ -263,7 +262,9 @@
     held[0:32, 128:256] = own_tail
 
     picked1 = jnp.where(scol[:32] < 32, scol[:32], -1000.0)
-    snd1[...] = dot(main_tail_rows(picked1, 32.0, 64), own2[...]).astype(BF16).reshape(4, 16, 128)
+    first_payload = dot(main_tail_rows(picked1, 32.0, 64), own2[...]) + named_tile(0)
+    snd1[...] = first_payload.astype(BF16).reshape(4, 16, 128)
+    second_names = named_tile(1)
 
     def exchange(rnd, snd, rcv, ss, rs):
         out = []
@@ -276,46 +277,47 @@
             out.append(c)
         return out
 
+    pl.semaphore_wait(barrier, 2 * (GROUP - 1))
     round1 = exchange(0, snd1, rcv1, ss1, rs1)
-
-    for c in table_copies:
-        c.wait_recv()
-    tabs[0] = tabrow[...]
-    tabs[GROUP] = tabrow[...]
-    rows1 = jnp.concatenate([tabs[m] for m in range(GROUP)], axis=0)
-    rows2 = jnp.concatenate([tabs[GROUP + m] for m in range(GROUP)], axis=0)
-    cols1 = jnp.transpose(jnp.concatenate([rows1, rows2] + [jnp.zeros((96, 128), F32)], axis=0))
-    from1 = routed(rows1, cols1[0:32, 0:16], 32.0)
-    from2 = routed(pltpu.roll(rows2, 96, 1), cols1[32:64, 16:32], 64.0)
+    up = pltpu.make_async_remote_copy(
+        src_ref=dup.at[pl.ds(BOXES, HALO)], dst_ref=dup.at[pl.ds(0, HALO)],
+        send_sem=hss.at[0], recv_sem=hrs.at[0], device_id={"gz": (gz + 1) % gzs}, device_id_type=MESH,
+    )
+    down = pltpu.make_async_remote_copy(
+        src_ref=dup.at[pl.ds(HALO, HALO)], dst_ref=dup.at[pl.ds(BOXES + HALO, HALO)],
+        send_sem=hss.at[1], recv_sem=hrs.at[1], device_id={"gz": (gz + gzs - 1) % gzs}, device_id_type=MESH,
+    )
+    up.start()
+    down.start()
+
     own_late = scol[32:64]
+    picked2 = jnp.where(own_late < 32, own_late, -1000.0)
+    from_own = dot(main_tail_rows(picked2, 32.0, 64), own2[...]) + second_names
     fwd = onehot(fiota((32, 32), 1) == own_late - 32.0).astype(BF16)
-    via = dot(fwd, jnp.broadcast_to(from1, (32, 128)).astype(BF16))[:, 0:1]
-    late = jnp.where(jnp.logical_and(own_late >= 32, own_late < 64), via, -1000.0)
-    lanes240 = fiota((32, 240), 1)
-    select1 = jnp.concatenate(
-        [
-            main_tail_rows(late, 8.0, 240),
-            onehot(lanes240 == from1).astype(BF16),
-            onehot(lanes240 == from1 + 8.0).astype(BF16),
-        ],
-        axis=0,
-    )
-    select2 = jnp.concatenate(
-        [onehot(lanes240 == from2).astype(BF16), onehot(lanes240 == from2 + 8.0).astype(BF16)], axis=0
-    )
-    picked2 = jnp.where(own_late < 32, own_late, -1000.0)
-    from_own = dot(main_tail_rows(picked2, 32.0, 64), own2[...])
-
-    up.wait_recv()
-    down.wait_recv()
+    loads[0].wait()
+    far_cols = far_ref[...].astype(F32).astype(BF16)
+    lanes96 = fiota((BOXES, 96), 1).astype(BF16)
+    for l in range(LIST):
+        here = jnp.where(lanes96 == far_cols[:, l : l + 1], jnp.ones((), BF16), jnp.zeros((), BF16))
+        oh[BOXES * l : BOXES * l + BOXES, :] = here
+
     base_box = (
         (lax.axis_index("gx") * lax.axis_size("gy") + lax.axis_index("gy")) * gzs + gz
     ) * BOXES - HALO
 
-    for e in range(EXT + 1):
+    def prepare(e):
         tile = dup[e]
         sources[e] = source_rows(tile).astype(BF16)
         charges[e] = jnp.broadcast_to(tile[3:4], (8, 128))
+
+    for e in list(range(HALO, BOXES + HALO)) + [EXT]:
+        prepare(e)
+    up.wait_recv()
+    down.wait_recv()
+    for e in list(range(HALO)) + list(range(BOXES + HALO, EXT)):
+        prepare(e)
+    loads[1].wait()
+    loads[2].wait()
 
     def near_box(g, _):
         lo = iota((8, 128), 1) < SLOTS
@@ -344,27 +346,41 @@
         accs[at, :] = jnp.concatenate(acc, axis=0)
         return 0
 
-    lax.fori_loop(0, BOXES // 2, near_box, 0, unroll=8)
+    lax.fori_loop(0, 8, near_box, 0, unroll=8)
 
     for c in round1:
         c.wait_recv()
+    lanes240 = fiota((32, 240), 1)
+    from1 = routed(rcv1, 0)
+    via = dot(fwd, jnp.broadcast_to(from1, (32, 128)).astype(BF16))[:, 0:1]
+    late = jnp.where(jnp.logical_and(own_late >= 32, own_late < 64), via, -1000.0)
+    select1 = jnp.concatenate(
+        [
+            main_tail_rows(late, 8.0, 240),
+            onehot(lanes240 == from1).astype(BF16),
+            onehot(lanes240 == from1 + 8.0).astype(BF16),
+        ],
+        axis=0,
+    )
     got = dot(select1, rcv1[...].reshape(240, 128))
-    snd2[...] = (got[0:64] + from_own).astype(BF16).reshape(4, 16, 128)
+    is_tail = iota((64, 128), 0) % 16 >= 8
+    passed_on = jnp.where(jnp.logical_and(is_tail, iota((64, 128), 1) >= 64), 0.0, got[0:64])
+    snd2[...] = (passed_on + from_own).astype(BF16).reshape(4, 16, 128)
     round2 = exchange(1, snd2, rcv2, ss2, rs2)
     held[32:64, 0:128] = got[64:96].astype(BF16)
     held[32:64, 128:256] = got[96:128].astype(BF16)
 
-    far_cols = far_ref[...].astype(F32)
-    lanes96 = fiota((BOXES, 96), 1)
-    for l in range(LIST):
-        oh[BOXES * l : BOXES * l + BOXES, :] = onehot(lanes96 == far_cols[0:BOXES, l : l + 1]).astype(BF16)
-    lax.fori_loop(BOXES // 2, BOXES, near_box, 0, unroll=8)
+    lax.fori_loop(8, BOXES, near_box, 0, unroll=8)
     ah, am = split2(accs[...])
     ones = jnp.ones((8, 128), BF16)
     near_row = (dot(ones, ah, NT) + dot(ones, am, NT))[0:1]
 
     for c in round2:
         c.wait_recv()
+    from2 = routed(rcv2, 1)
+    select2 = jnp.concatenate(
+        [onehot(lanes240 == from2).astype(BF16), onehot(lanes240 == from2 + 8.0).astype(BF16)], axis=0
+    )
     got2 = dot(select2, rcv2[...].reshape(240, 128))
     held[64:96, 0:128] = got2[0:32].astype(BF16)
     held[64:96, 128:256] = got2[32:64].astype(BF16)
@@ -394,7 +410,7 @@
             out_ref[:, 128 * r : 128 * r + 128] = jnp.where(
                 slot_in_box < count, both[:, 128 * h : 128 * h + 128], 0.0
             )
-    for c in table_copies + round1 + round2 + [up, down]:
+    for c in round1 + round2 + [up, down]:
         c.wait_send()
 
 
@@ -413,11 +429,12 @@
 def local_part(leaf_offsets, latent_charges, atom_counts, near_boxes, far_slots, branch_slots, far_operators):
     vmem = pl.BlockSpec(memory_space=pltpu.VMEM)
     smem = pl.BlockSpec(memory_space=pltpu.SMEM)
+    hbm = pl.BlockSpec(memory_space=pl.ANY)
     sem = pltpu.SemaphoreType.DMA
     out = pl.pallas_call(
         kernel,
         out_shape=jax.ShapeDtypeStruct((1, ATOMS), F32),
-        in_specs=[vmem, vmem, smem, smem, vmem, vmem, pl.BlockSpec(memory_space=pl.ANY), vmem],
+        in_specs=[vmem, vmem, smem, hbm, hbm, vmem, hbm, hbm],
         out_specs=vmem,
         scratch_shapes=[
             pltpu.VMEM((TERMS, LIST * TERMS), BF16),
@@ -428,8 +445,9 @@
             pltpu.VMEM((EXT + 1, 48, 128), BF16),
             pltpu.VMEM((EXT + 1, 8, 128), F32),
             pltpu.VMEM((ATOMS, 128), F32),
-            pltpu.VMEM((1, 128), F32),
-            pltpu.VMEM((2 * GROUP, 1, 128), F32),
+            pltpu.SMEM((len(SHIFTS) - 2, BOXES), jnp.int32),
+            pltpu.VMEM((BOXES, LIST), jnp.int32),
+            pltpu.VMEM((PAIRS, 48, 128), BF16),
             pltpu.VMEM((64, 128), BF16),
             pltpu.VMEM((4, 16, 128), BF16),
             pltpu.VMEM((4, 16, 128), BF16),
@@ -440,8 +458,7 @@
             pltpu.VMEM((BOXES, 31232), BF16),
             pltpu.VMEM((BOXES, 128), F32),
             sem,
-            sem((2 * GROUP,)),
-            sem((2 * GROUP,)),
+            sem((3,)),
             sem((2,)),
             sem((2,)),
             sem((GROUP - 1,)),

time: 34.3 us -> 31.1 us (0.907)
  Pallas kernels: 32.8 us -> 29.6 us
    pallas_call x1, Pallas kernels: 32.8 us -> 29.6 us  [local_part(): pl.pallas_call(kernel, out_shape=jax.ShapeDtypeStruct((1, ATOMS), F32), i...]
where the time goes in v3:
time: 31.1 us; the launch traced here: 30.9 us
  Pallas kernels  29.6 us (95%)
  local copies, waits for them, and re-layouts  1.3 us (4%)
    pallas_call x1, Pallas kernels, local_part(): pl.pallas_call(kernel, out_shape=jax.ShapeDtypeStruct((1, ATOMS), F32), i...  29.6 us
    unnamed x1, local copies, waits for them, and re-layouts  1.3 us

profile of v3, /device:TPU:1, one launch (start us, length us, event | category | flops | bytes accessed | tf_op | source)
XLA Modules:
  0.0 30.9 jit_solution(18046137948652292745)
XLA Ops:
  0.0 29.6 %shard_map.82 = f32[1,2048]{1,0:T(1,128)} custom-call(f32[3,2048]{1,0:T(4,128)} %offs_ref.1, f32[1,2048]{1,0:T(1,128)} %bitcast.5, s32[32]{0:T(128)} %counts_ref.1, s32[26,32]{1,0:T(8,128)} %near_hbm.1, s32[32,189]{1,0:T(8,128)} %bitcast.3, s32[1,8,8]{2,1,0:T(8,128)} %branch_ref.1, bf16[165,31185]{1,0:T(8,128)(2,1)} %op_hbm.1, ...), custom_call_target="tpu_custom_call" | custom-call | tf_op jit(solution)/shard_map/pallas_call | solution.py:434
  29.6 1.3 %copy.10 = f32[2048]{0:T(1024)} copy(f32[2048]{0:T(1024)} %bitcast.4) | data formatting | bytes 16384

commit v4 on v3

--- a/solution.py
+++ b/solution.py
@@ -25,6 +25,10 @@
 MESH = pl.DeviceIdType.MESH
 SHIFTS = [s for s in itertools.product((-1, 0, 1), repeat=3) if s != (0, 0, 0)] + [(0, 0, 0)] * 2
 PAIRS = len(SHIFTS) // 2
+FARTHEST = (
+    (8, 9, 10, 11, 6, 7, 12, 13, 4, 5, 14, 15, 2, 3, 1),
+    (10, 6, 14, 9, 11, 2, 8, 5, 7, 13, 15, 1, 3, 4, 12),
+)
 
 
 def degree_start(n):
@@ -173,24 +177,38 @@
 
 
 def kernel(
-    offs_ref, q_ref, counts_ref, near_hbm, far_hbm, branch_ref, op_hbm, factor_hbm, out_ref,
-    opv, tv, p8, dup, aims, sources, charges, accs, near_ref, far_ref, factor_ref, own2, snd1, snd2, rcv1, rcv2, held, oh, col, tail,
+    offs_hbm, q_hbm, counts_hbm, near_hbm, far_hbm, branch_hbm, op_hbm, factor_hbm, near_out, far_out,
+    opv, tv, p8, dup, aims, sources, charges, accs, offs_ref, q_ref, counts_ref, branch_ref, near_ref, far_ref, factor_ref, own2, snd1, snd2, rcv1, rcv2, held, oh, col, tail,
     op_sem, in_sems, hss, hrs, ss1, rs1, ss2, rs2,
 ):
+    gz = lax.axis_index("gz")
+    gzs = lax.axis_size("gz")
+    barrier = pltpu.get_barrier_semaphore()
     loads = [
         pltpu.make_async_copy(src, dst, in_sems.at[i])
-        for i, (src, dst) in enumerate(((far_hbm, far_ref), (near_hbm, near_ref), (factor_hbm, factor_ref)))
+        for i, (src, dst) in enumerate(
+            (
+                (offs_hbm, offs_ref),
+                (q_hbm, q_ref),
+                (counts_hbm, counts_ref),
+                (branch_hbm, branch_ref),
+                (far_hbm, far_ref),
+                (near_hbm, near_ref),
+                (factor_hbm, factor_ref),
+            )
+        )
     ]
-    for c in loads:
+    for c in loads[:4]:
+        c.start()
+    for rnd in range(2):
+        for m in FARTHEST[rnd]:
+            pl.semaphore_signal(barrier, inc=1, device_id=partner(rnd, m), device_id_type=MESH)
+    for c in loads[4:]:
         c.start()
     op_copy = pltpu.make_async_copy(op_hbm, opv, op_sem)
     op_copy.start()
-    gz = lax.axis_index("gz")
-    gzs = lax.axis_size("gz")
-    barrier = pltpu.get_barrier_semaphore()
-    for rnd in range(2):
-        for m in range(1, GROUP):
-            pl.semaphore_signal(barrier, inc=1, device_id=partner(rnd, m), device_id_type=MESH)
+    for c in loads[:4]:
+        c.wait()
 
     lo8 = iota((8, 128), 1) < SLOTS
     slot_in_box = iota((1, 128), 1) % SLOTS
@@ -268,7 +286,7 @@
 
     def exchange(rnd, snd, rcv, ss, rs):
         out = []
-        for m in range(1, GROUP):
+        for m in FARTHEST[rnd]:
             c = pltpu.make_async_remote_copy(
                 src_ref=snd.at[low(m)], dst_ref=rcv.at[m - 1], send_sem=ss.at[m - 1], recv_sem=rs.at[m - 1],
                 device_id=partner(rnd, m), device_id_type=MESH,
@@ -294,7 +312,7 @@
     picked2 = jnp.where(own_late < 32, own_late, -1000.0)
     from_own = dot(main_tail_rows(picked2, 32.0, 64), own2[...]) + second_names
     fwd = onehot(fiota((32, 32), 1) == own_late - 32.0).astype(BF16)
-    loads[0].wait()
+    loads[4].wait()
     far_cols = far_ref[...].astype(F32).astype(BF16)
     lanes96 = fiota((BOXES, 96), 1).astype(BF16)
     for l in range(LIST):
@@ -316,8 +334,8 @@
     down.wait_recv()
     for e in list(range(HALO)) + list(range(BOXES + HALO, EXT)):
         prepare(e)
-    loads[1].wait()
-    loads[2].wait()
+    loads[5].wait()
+    loads[6].wait()
 
     def near_box(g, _):
         lo = iota((8, 128), 1) < SLOTS
@@ -346,7 +364,7 @@
         accs[at, :] = jnp.concatenate(acc, axis=0)
         return 0
 
-    lax.fori_loop(0, 8, near_box, 0, unroll=8)
+    lax.fori_loop(0, 16, near_box, 0, unroll=8)
 
     for c in round1:
         c.wait_recv()
@@ -370,10 +388,13 @@
     held[32:64, 0:128] = got[64:96].astype(BF16)
     held[32:64, 128:256] = got[96:128].astype(BF16)
 
-    lax.fori_loop(8, BOXES, near_box, 0, unroll=8)
+    lax.fori_loop(16, BOXES, near_box, 0, unroll=8)
     ah, am = split2(accs[...])
     ones = jnp.ones((8, 128), BF16)
     near_row = (dot(ones, ah, NT) + dot(ones, am, NT))[0:1]
+    for r in range(BOXES // 2):
+        count = jnp.where(lo1, counts_ref[2 * r], counts_ref[2 * r + 1])
+        near_out[r : r + 1, :] = jnp.where(slot_in_box < count, near_row[:, 128 * r : 128 * r + 128], 0.0)
 
     for c in round2:
         c.wait_recv()
@@ -403,13 +424,10 @@
         boxes = onehot((256 * blk + iota((96, 256), 1)) // SLOTS == iota((96, 256), 0) % BOXES).astype(BF16)
         there = dot(parts, boxes)
         far = jnp.sum(there * tv[0:TERMS, span], axis=0, keepdims=True)
-        both = far + near_row[:, span]
         for h in range(2):
             r = 2 * blk + h
             count = jnp.where(lo1, counts_ref[2 * r], counts_ref[2 * r + 1])
-            out_ref[:, 128 * r : 128 * r + 128] = jnp.where(
-                slot_in_box < count, both[:, 128 * h : 128 * h + 128], 0.0
-            )
+            far_out[r : r + 1, :] = jnp.where(slot_in_box < count, far[:, 128 * h : 128 * h + 128], 0.0)
     for c in round1 + round2 + [up, down]:
         c.wait_send()
 
@@ -428,14 +446,13 @@
 
 def local_part(leaf_offsets, latent_charges, atom_counts, near_boxes, far_slots, branch_slots, far_operators):
     vmem = pl.BlockSpec(memory_space=pltpu.VMEM)
-    smem = pl.BlockSpec(memory_space=pltpu.SMEM)
     hbm = pl.BlockSpec(memory_space=pl.ANY)
     sem = pltpu.SemaphoreType.DMA
-    out = pl.pallas_call(
+    near, far = pl.pallas_call(
         kernel,
-        out_shape=jax.ShapeDtypeStruct((1, ATOMS), F32),
-        in_specs=[vmem, vmem, smem, hbm, hbm, vmem, hbm, hbm],
-        out_specs=vmem,
+        out_shape=[jax.ShapeDtypeStruct((ATOMS // 128, 128), F32)] * 2,
+        in_specs=[hbm] * 8,
+        out_specs=[vmem, vmem],
         scratch_shapes=[
             pltpu.VMEM((TERMS, LIST * TERMS), BF16),
             pltpu.VMEM((ROWS, ATOMS), F32),
@@ -445,6 +462,10 @@
             pltpu.VMEM((EXT + 1, 48, 128), BF16),
             pltpu.VMEM((EXT + 1, 8, 128), F32),
             pltpu.VMEM((ATOMS, 128), F32),
+            pltpu.VMEM((3, ATOMS), F32),
+            pltpu.VMEM((1, ATOMS), F32),
+            pltpu.SMEM((BOXES,), jnp.int32),
+            pltpu.VMEM((1, 8, 8), jnp.int32),
             pltpu.SMEM((len(SHIFTS) - 2, BOXES), jnp.int32),
             pltpu.VMEM((BOXES, LIST), jnp.int32),
             pltpu.VMEM((PAIRS, 48, 128), BF16),
@@ -458,7 +479,7 @@
             pltpu.VMEM((BOXES, 31232), BF16),
             pltpu.VMEM((BOXES, 128), F32),
             sem,
-            sem((3,)),
+            sem((7,)),
             sem((2,)),
             sem((2,)),
             sem((GROUP - 1,)),
@@ -479,7 +500,7 @@
         far_operators,
         factor_tiles(),
     )
-    return out.reshape(-1)
+    return (near + far).reshape(-1)
 
 
 def solution(mesh):

time: 31.1 us -> 31.1 us (level)
  other arithmetic: 0 us -> 1.32 us
  local copies, waits for them, and re-layouts: 1.3 us -> 0 us
    reshape x0 -> x1, other arithmetic: none -> 1.32 us  [local_part(): return (near + far).reshape(-1)]
    unnamed x1 -> x0, local copies, waits for them, and re-layouts: 1.3 us -> none
where the time goes in v4:
time: 31.1 us; the launch traced here: 31 us
  Pallas kernels  29.7 us (95%)
  other arithmetic  1.32 us (4%)
    pallas_call x1, Pallas kernels, local_part(): pl.pallas_call(kernel, out_shape=[jax.ShapeDtypeStruct((ATOMS // 128, 128...  29.7 us
    reshape x1, other arithmetic, local_part(): return (near + far).reshape(-1)  1.32 us

profile of v4, /device:TPU:1, one launch (start us, length us, event | category | flops | bytes accessed | tf_op | source)
XLA Modules:
  0.0 31.0 jit_solution(18266703060211509314)
XLA Ops:
  0.0 29.7 %shard_map.82 = (f32[16,128]{1,0:T(8,128)}, f32[16,128]{1,0:T(8,128)}) custom-call(f32[3,2048]{1,0:T(4,128)} %offs_hbm.1, f32[1,2048]{1,0:T(1,128)} %bitcast.5, s32[32]{0:T(128)} %counts_hbm.1, s32[26,32]{1,0:T(8,128)} %near_hbm.1, s32[32,189]{1,0:T(8,128)} %bitcast.4, s32[1,8,8]{2,1,0:T(8,128)} %branch_hbm.1, bf16[165,31185]{1,0:T(8,128)(2,1)} %op_hbm.1, ...), custom_call_target="tpu_custom_call" | custom-call | tf_op jit(solution)/shard_map/pallas_call | solution.py:451
  29.7 1.3 %add_bitcast_fusion = f32[2048]{0:T(1024)} fusion(f32[16,128]{1,0:T(8,128)} %get-tuple-element.7, f32[16,128]{1,0:T(8,128)} %get-tuple-element.8), kind=kLoop, calls=%fused_computation | loop fusion | flops 2048 | bytes 24576 | tf_op jit(solution)/shard_map/reshape | solution.py:503

commit v5 on v4

--- a/solution.py
+++ b/solution.py
@@ -39,20 +39,17 @@
     return (m & -m).bit_length() - 1
 
 
-def flipped(v, mask, bits):
-    for b in range(bits):
+def flips(axis, bits):
+    at = lax.axis_index(axis)
+    return [(1 << b) * (1 - 2 * lax.rem(lax.div(at, jnp.int32(1 << b)), jnp.int32(2))) for b in range(bits)]
+
+
+def moved(axis, steps, mask):
+    at = lax.axis_index(axis)
+    for b, step in enumerate(steps):
         if mask >> b & 1:
-            v = v + (1 << b) - (2 << b) * ((v // (1 << b)) % 2)
-    return v
-
-
-def partner(rnd, m):
-    if rnd == 0:
-        return {"gz": flipped(lax.axis_index("gz"), m, 4)}
-    return {
-        "gy": flipped(lax.axis_index("gy"), m & 3, 2),
-        "gx": flipped(lax.axis_index("gx"), m >> 2, 2),
-    }
+            at = at + step
+    return at
 
 
 def iota(shape, dim):
@@ -183,6 +180,11 @@
 ):
     gz = lax.axis_index("gz")
     gzs = lax.axis_size("gz")
+    z_flips, y_flips, x_flips = flips("gz", 4), flips("gy", 2), flips("gx", 2)
+    at_gz = [{"gz": moved("gz", z_flips, m)} for m in range(GROUP)]
+    at_gy = [moved("gy", y_flips, m) for m in range(4)]
+    at_gx = [moved("gx", x_flips, m) for m in range(4)]
+    partners = (at_gz, [{"gy": at_gy[m & 3], "gx": at_gx[m >> 2]} for m in range(GROUP)])
     barrier = pltpu.get_barrier_semaphore()
     loads = [
         pltpu.make_async_copy(src, dst, in_sems.at[i])
@@ -202,7 +204,7 @@
         c.start()
     for rnd in range(2):
         for m in FARTHEST[rnd]:
-            pl.semaphore_signal(barrier, inc=1, device_id=partner(rnd, m), device_id_type=MESH)
+            pl.semaphore_signal(barrier, inc=1, device_id=partners[rnd][m], device_id_type=MESH)
     for c in loads[4:]:
         c.start()
     op_copy = pltpu.make_async_copy(op_hbm, opv, op_sem)
@@ -289,7 +291,7 @@
         for m in FARTHEST[rnd]:
             c = pltpu.make_async_remote_copy(
                 src_ref=snd.at[low(m)], dst_ref=rcv.at[m - 1], send_sem=ss.at[m - 1], recv_sem=rs.at[m - 1],
-                device_id=partner(rnd, m), device_id_type=MESH,
+                device_id=partners[rnd][m], device_id_type=MESH,
             )
             c.start()
             out.append(c)
@@ -299,11 +301,11 @@
     round1 = exchange(0, snd1, rcv1, ss1, rs1)
     up = pltpu.make_async_remote_copy(
         src_ref=dup.at[pl.ds(BOXES, HALO)], dst_ref=dup.at[pl.ds(0, HALO)],
-        send_sem=hss.at[0], recv_sem=hrs.at[0], device_id={"gz": (gz + 1) % gzs}, device_id_type=MESH,
+        send_sem=hss.at[0], recv_sem=hrs.at[0], device_id={"gz": lax.rem(gz + 1, gzs)}, device_id_type=MESH,
     )
     down = pltpu.make_async_remote_copy(
         src_ref=dup.at[pl.ds(HALO, HALO)], dst_ref=dup.at[pl.ds(BOXES + HALO, HALO)],
-        send_sem=hss.at[1], recv_sem=hrs.at[1], device_id={"gz": (gz + gzs - 1) % gzs}, device_id_type=MESH,
+        send_sem=hss.at[1], recv_sem=hrs.at[1], device_id={"gz": lax.rem(gz + gzs - 1, gzs)}, device_id_type=MESH,
     )
     up.start()
     down.start()
@@ -364,7 +366,7 @@
         accs[at, :] = jnp.concatenate(acc, axis=0)
         return 0
 
-    lax.fori_loop(0, 16, near_box, 0, unroll=8)
+    lax.fori_loop(0, 8, near_box, 0, unroll=8)
 
     for c in round1:
         c.wait_recv()
@@ -388,7 +390,7 @@
     held[32:64, 0:128] = got[64:96].astype(BF16)
     held[32:64, 128:256] = got[96:128].astype(BF16)
 
-    lax.fori_loop(16, BOXES, near_box, 0, unroll=8)
+    lax.fori_loop(8, BOXES, near_box, 0, unroll=8)
     ah, am = split2(accs[...])
     ones = jnp.ones((8, 128), BF16)
     near_row = (dot(ones, ah, NT) + dot(ones, am, NT))[0:1]

time: 31.1 us -> 30 us (0.965)
  Pallas kernels: 29.7 us -> 28.5 us
    pallas_call x1, Pallas kernels: 29.7 us -> 28.5 us  [local_part(): pl.pallas_call(kernel, out_shape=[jax.ShapeDtypeStruct((ATOMS // 128, 128...]
where the time goes in v5:
time: 30 us; the launch traced here: 29.8 us
  Pallas kernels  28.5 us (95%)
  other arithmetic  1.32 us (4%)
    pallas_call x1, Pallas kernels, local_part(): pl.pallas_call(kernel, out_shape=[jax.ShapeDtypeStruct((ATOMS // 128, 128...  28.5 us
    reshape x1, other arithmetic, local_part(): return (near + far).reshape(-1)  1.32 us

profile of v5, /device:TPU:1, one launch (start us, length us, event | category | flops | bytes accessed | tf_op | source)
XLA Modules:
  0.0 29.8 jit_solution(16611556568171202486)
XLA Ops:
  0.0 28.5 %shard_map.82 = (f32[16,128]{1,0:T(8,128)}, f32[16,128]{1,0:T(8,128)}) custom-call(f32[3,2048]{1,0:T(4,128)} %offs_hbm.1, f32[1,2048]{1,0:T(1,128)} %bitcast.5, s32[32]{0:T(128)} %counts_hbm.1, s32[26,32]{1,0:T(8,128)} %near_hbm.1, s32[32,189]{1,0:T(8,128)} %bitcast.4, s32[1,8,8]{2,1,0:T(8,128)} %branch_hbm.1, bf16[165,31185]{1,0:T(8,128)(2,1)} %op_hbm.1, ...), custom_call_target="tpu_custom_call" | custom-call | tf_op jit(solution)/shard_map/pallas_call | solution.py:453
  28.5 1.3 %add_bitcast_fusion = f32[2048]{0:T(1024)} fusion(f32[16,128]{1,0:T(8,128)} %get-tuple-element.7, f32[16,128]{1,0:T(8,128)} %get-tuple-element.8), kind=kLoop, calls=%fused_computation | loop fusion | flops 2048 | bytes 24576 | tf_op jit(solution)/shard_map/reshape | solution.py:505

commit v6 on v5

--- a/solution.py
+++ b/solution.py
@@ -174,7 +174,7 @@
 
 
 def kernel(
-    offs_hbm, q_hbm, counts_hbm, near_hbm, far_hbm, branch_hbm, op_hbm, factor_hbm, near_out, far_out,
+    offs_hbm, q_hbm, counts_hbm, near_hbm, far_hbm, branch_hbm, op_hbm, factor_hbm, out_ref,
     opv, tv, p8, dup, aims, sources, charges, accs, offs_ref, q_ref, counts_ref, branch_ref, near_ref, far_ref, factor_ref, own2, snd1, snd2, rcv1, rcv2, held, oh, col, tail,
     op_sem, in_sems, hss, hrs, ss1, rs1, ss2, rs2,
 ):
@@ -396,7 +396,7 @@
     near_row = (dot(ones, ah, NT) + dot(ones, am, NT))[0:1]
     for r in range(BOXES // 2):
         count = jnp.where(lo1, counts_ref[2 * r], counts_ref[2 * r + 1])
-        near_out[r : r + 1, :] = jnp.where(slot_in_box < count, near_row[:, 128 * r : 128 * r + 128], 0.0)
+        out_ref[r : r + 1, :] = jnp.where(slot_in_box < count, near_row[:, 128 * r : 128 * r + 128], 0.0)
 
     for c in round2:
         c.wait_recv()
@@ -429,7 +429,8 @@
         for h in range(2):
             r = 2 * blk + h
             count = jnp.where(lo1, counts_ref[2 * r], counts_ref[2 * r + 1])
-            far_out[r : r + 1, :] = jnp.where(slot_in_box < count, far[:, 128 * h : 128 * h + 128], 0.0)
+            here = jnp.where(slot_in_box < count, far[:, 128 * h : 128 * h + 128], 0.0)
+            out_ref[r : r + 1, :] = out_ref[r : r + 1, :] + here
     for c in round1 + round2 + [up, down]:
         c.wait_send()
 
@@ -450,11 +451,11 @@
     vmem = pl.BlockSpec(memory_space=pltpu.VMEM)
     hbm = pl.BlockSpec(memory_space=pl.ANY)
     sem = pltpu.SemaphoreType.DMA
-    near, far = pl.pallas_call(
+    out = pl.pallas_call(
         kernel,
-        out_shape=[jax.ShapeDtypeStruct((ATOMS // 128, 128), F32)] * 2,
+        out_shape=jax.ShapeDtypeStruct((ATOMS // 128, 128), F32),
         in_specs=[hbm] * 8,
-        out_specs=[vmem, vmem],
+        out_specs=vmem,
         scratch_shapes=[
             pltpu.VMEM((TERMS, LIST * TERMS), BF16),
             pltpu.VMEM((ROWS, ATOMS), F32),
@@ -502,7 +503,7 @@
         far_operators,
         factor_tiles(),
     )
-    return (near + far).reshape(-1)
+    return out.reshape(-1)
 
 
 def solution(mesh):

time: 30 us -> 30 us (level)
  other arithmetic: 1.32 us -> 0 us
  local copies, waits for them, and re-layouts: 0 us -> 1.3 us
    reshape x1 -> x0, other arithmetic: 1.32 us -> none  [local_part(): return (near + far).reshape(-1)]
    unnamed x0 -> x1, local copies, waits for them, and re-layouts: none -> 1.3 us
where the time goes in v6:
time: 30 us; the launch traced here: 29.8 us
  Pallas kernels  28.5 us (95%)
  local copies, waits for them, and re-layouts  1.3 us (4%)
    pallas_call x1, Pallas kernels, local_part(): pl.pallas_call(kernel, out_shape=jax.ShapeDtypeStruct((ATOMS // 128, 128)...  28.5 us
    unnamed x1, local copies, waits for them, and re-layouts  1.3 us

profile of v6, /device:TPU:1, one launch (start us, length us, event | category | flops | bytes accessed | tf_op | source)
XLA Modules:
  0.0 29.8 jit_solution(4807678861387556140)
XLA Ops:
  0.0 28.5 %shard_map.82 = f32[16,128]{1,0:T(8,128)} custom-call(f32[3,2048]{1,0:T(4,128)} %offs_hbm.1, f32[1,2048]{1,0:T(1,128)} %bitcast.5, s32[32]{0:T(128)} %counts_hbm.1, s32[26,32]{1,0:T(8,128)} %near_hbm.1, s32[32,189]{1,0:T(8,128)} %bitcast.3, s32[1,8,8]{2,1,0:T(8,128)} %branch_hbm.1, bf16[165,31185]{1,0:T(8,128)(2,1)} %op_hbm.1, ...), custom_call_target="tpu_custom_call" | custom-call | tf_op jit(solution)/shard_map/pallas_call | solution.py:454
  28.5 1.3 %copy.10 = f32[2048]{0:T(1024)} copy(f32[2048]{0:T(1024)} %bitcast.4) | data formatting | bytes 16384

commit v7 on v5

--- a/solution.py
+++ b/solution.py
@@ -260,7 +260,7 @@
         tv[TERMS:ROWS, span] = jnp.zeros((ROWS - TERMS, 256), F32)
         return 0
 
-    lax.fori_loop(0, ATOMS // 256, terms_block, 0)
+    lax.fori_loop(0, ATOMS // 256, terms_block, 0, unroll=4)
 
     head = jnp.zeros((64, ROWS), F32)
     rest = jnp.zeros((32, ROWS), F32)
@@ -390,7 +390,7 @@
     held[32:64, 0:128] = got[64:96].astype(BF16)
     held[32:64, 128:256] = got[96:128].astype(BF16)
 
-    lax.fori_loop(8, BOXES, near_box, 0, unroll=8)
+    lax.fori_loop(8, BOXES, near_box, 0, unroll=12)
     ah, am = split2(accs[...])
     ones = jnp.ones((8, 128), BF16)
     near_row = (dot(ones, ah, NT) + dot(ones, am, NT))[0:1]

time: 30 us -> 30 us (level)
  no operation moved by 1% of the time
where the time goes in v7:
time: 30 us; the launch traced here: 29.8 us
  Pallas kernels  28.5 us (95%)
  other arithmetic  1.32 us (4%)
    pallas_call x1, Pallas kernels, local_part(): pl.pallas_call(kernel, out_shape=[jax.ShapeDtypeStruct((ATOMS // 128, 128...  28.5 us
    reshape x1, other arithmetic, local_part(): return (near + far).reshape(-1)  1.32 us

profile of v7, /device:TPU:1, one launch (start us, length us, event | category | flops | bytes accessed | tf_op | source)
XLA Modules:
  0.0 29.8 jit_solution(1613663269578166465)
XLA Ops:
  0.0 28.5 %shard_map.82 = (f32[16,128]{1,0:T(8,128)}, f32[16,128]{1,0:T(8,128)}) custom-call(f32[3,2048]{1,0:T(4,128)} %offs_hbm.1, f32[1,2048]{1,0:T(1,128)} %bitcast.5, s32[32]{0:T(128)} %counts_hbm.1, s32[26,32]{1,0:T(8,128)} %near_hbm.1, s32[32,189]{1,0:T(8,128)} %bitcast.4, s32[1,8,8]{2,1,0:T(8,128)} %branch_hbm.1, bf16[165,31185]{1,0:T(8,128)(2,1)} %op_hbm.1, ...), custom_call_target="tpu_custom_call" | custom-call | tf_op jit(solution)/shard_map/pallas_call | solution.py:453
  28.5 1.3 %add_bitcast_fusion = f32[2048]{0:T(1024)} fusion(f32[16,128]{1,0:T(8,128)} %get-tuple-element.7, f32[16,128]{1,0:T(8,128)} %get-tuple-element.8), kind=kLoop, calls=%fused_computation | loop fusion | flops 2048 | bytes 24576 | tf_op jit(solution)/shard_map/reshape | solution.py:505
